TPU v7x, 512 devices: a whole 4x4x16 slice. The times are simulated.
512 devices in a mesh: expert: 8 (over y, core), tensor: 64 (over x, z).
Axes of the slice: x: 4, y: 4, z: 16, core: 2. Of those that a mesh axis runs over, the one named last changes fastest.
Arguments:
- tokens: bfloat16 [1024, 2048], P('expert', 'tensor'), may hold values from -6 to 6
- out_grad: bfloat16 [1024, 2048], P('expert', 'tensor'), may hold values from -3 to 3
- routes: int32 [1024, 2], P('expert'), may hold values from 0 to 7, all different within a row; in each aligned block of 128 rows (0 to 127, 128 to 255, ...) at most 64 rows name the same one
- gate_values: bfloat16 [1024, 2], P('expert'), may hold values from 0.049804688 to 0.94921875
- gate_weight: bfloat16 [8, 2048, 8192], P('expert', None, 'tensor'), may hold values from -0.125 to 0.125
- up_weight: bfloat16 [8, 2048, 8192], P('expert', None, 'tensor'), may hold values from -0.125 to 0.125
- down_weight: bfloat16 [8, 8192, 2048], P('expert', 'tensor'), may hold values from -0.0625 to 0.0625
Outputs:
- tokens_grad: bfloat16 [1024, 2048], P('expert', 'tensor')
- gate_values_grad: float32 [1024, 2], P('expert')
- gate_weight_grad: bfloat16 [8, 2048, 8192], P('expert', None, 'tensor')
- up_weight_grad: bfloat16 [8, 2048, 8192], P('expert', None, 'tensor')
- down_weight_grad: bfloat16 [8, 8192, 2048], P('expert', 'tensor')
Inputs may be any that keep to these rules, and one draw needn't show every extreme that they name: `routes`: each token names 2 different experts. Among the 128 tokens of one index of the expert axis no expert is named by more than 64 of them, and in some such block one expert is named by exactly 64.
All inputs are finite; a program needn't handle non-finite values.
Results may differ from a plain program's by a relative error of at most 0.005.
Values may be sent and summed in bfloat16 or wider, within the bound.
A program may use at most 64 MiB of HBM per device.

v0:
```python
import jax
import jax.numpy as jnp
from jax import lax
from jax.sharding import PartitionSpec as P

contract_cols = (((1,), (1,)), ((), ()))
contract_rows = (((0,), (0,)), ((), ()))


def silu_parts(pre_gate):
    sigmoid_gate = jax.nn.sigmoid(pre_gate)
    activated = pre_gate * sigmoid_gate
    slope = sigmoid_gate * (1.0 + pre_gate * (1.0 - sigmoid_gate))
    return (activated, slope)


def slot_table(routes, expert_count, capacity):
    flat_routes = routes.reshape(-1)
    labels = jnp.arange(expert_count, dtype=jnp.int32)
    chosen = (flat_routes[:, None] == labels[None, :]).astype(jnp.int32)
    before = jnp.cumsum(chosen, axis=0) - chosen
    position = jnp.sum(before * chosen, axis=1)
    target = flat_routes * capacity + position
    slot_ids = jnp.arange(expert_count * capacity, dtype=jnp.int32)
    return (slot_ids[:, None] == target[None, :]).astype(jnp.float32)


def send_rows(pair_table, token_count, top_count, source_rows, source_grads, gate_values):
    slot_count = pair_table.shape[0]
    token_table = jnp.sum(pair_table.reshape(slot_count, token_count, top_count), axis=2).astype(
        jnp.bfloat16
    )
    pair_half = pair_table.astype(jnp.bfloat16)
    rows_out = jnp.dot(token_table, source_rows, preferred_element_type=jnp.float32).astype(
        jnp.bfloat16
    )
    grads_out = jnp.dot(token_table, source_grads, preferred_element_type=jnp.float32).astype(
        jnp.bfloat16
    )
    values_out = jnp.dot(
        pair_half, gate_values.reshape(-1), preferred_element_type=jnp.float32
    ).astype(jnp.bfloat16)
    return (rows_out, grads_out, values_out)


def finish(pre_gate, pre_up, hidden_grad, weights):
    activated, slope = silu_parts(pre_gate)
    gate_partial = jnp.sum(activated * pre_up * hidden_grad, axis=1)
    scaled_hidden = (weights[:, None] * activated * pre_up).astype(jnp.bfloat16)
    gate_pre_grad = (weights[:, None] * hidden_grad * pre_up * slope).astype(jnp.bfloat16)
    up_pre_grad = (weights[:, None] * hidden_grad * activated).astype(jnp.bfloat16)
    return (gate_partial, scaled_hidden, gate_pre_grad, up_pre_grad)


def from_whole(rows_whole, grads_whole, weights, gate_local, up_local, down_local):
    pre_gate = jnp.dot(rows_whole, gate_local, preferred_element_type=jnp.float32)
    pre_up = jnp.dot(rows_whole, up_local, preferred_element_type=jnp.float32)
    hidden_grad = lax.dot_general(
        grads_whole, down_local, contract_cols, preferred_element_type=jnp.float32
    )
    gate_partial, scaled_hidden, gate_pre_grad, up_pre_grad = finish(
        pre_gate, pre_up, hidden_grad, weights
    )
    gate_grad = lax.dot_general(
        rows_whole, gate_pre_grad, contract_rows, preferred_element_type=jnp.float32
    ).astype(jnp.bfloat16)
    up_grad = lax.dot_general(
        rows_whole, up_pre_grad, contract_rows, preferred_element_type=jnp.float32
    ).astype(jnp.bfloat16)
    down_grad = lax.dot_general(
        scaled_hidden, grads_whole, contract_rows, preferred_element_type=jnp.float32
    ).astype(jnp.bfloat16)
    return (gate_partial, gate_pre_grad, up_pre_grad, gate_grad, up_grad, down_grad)


def per_device(tokens, out_grad, routes, gate_values, gate_weight, up_weight, down_weight):
    expert_count = lax.axis_size("expert")
    token_count, top_count = routes.shape
    capacity = min(token_count, 4 * token_count // expert_count)
    slot_count = expert_count * capacity
    feat_local = tokens.shape[1]
    gate_local = gate_weight[0]
    up_local = up_weight[0]
    down_local = down_weight[0]
    pair_table = slot_table(routes, expert_count, capacity)
    rows_out, grads_out, values_out = send_rows(
        pair_table, token_count, top_count, tokens, out_grad, gate_values
    )
    rows_in, grads_in, values_in = (
        lax.all_to_all(
            rows_out.reshape(expert_count, capacity, feat_local),
            "expert",
            split_axis=0,
            concat_axis=0,
            tiled=True,
        ),
        lax.all_to_all(
            grads_out.reshape(expert_count, capacity, feat_local),
            "expert",
            split_axis=0,
            concat_axis=0,
            tiled=True,
        ),
        lax.all_to_all(
            values_out.reshape(expert_count, capacity),
            "expert",
            split_axis=0,
            concat_axis=0,
            tiled=True,
        ),
    )
    rows_in = rows_in.reshape(slot_count, feat_local)
    grads_in = grads_in.reshape(slot_count, feat_local)
    weights = values_in.reshape(slot_count).astype(jnp.float32)
    rows_whole, grads_whole = (
        lax.all_gather(rows_in, "tensor", axis=1, tiled=True),
        lax.all_gather(grads_in, "tensor", axis=1, tiled=True),
    )
    gate_partial, gate_pre_grad, up_pre_grad, gate_grad, up_grad, down_grad = from_whole(
        rows_whole, grads_whole, weights, gate_local, up_local, down_local
    )
    gate_sums = lax.psum(gate_partial, "tensor")
    input_part = lax.psum_scatter(
        lax.dot_general(
            gate_local, gate_pre_grad, contract_cols, preferred_element_type=jnp.float32
        )
        + lax.dot_general(up_local, up_pre_grad, contract_cols, preferred_element_type=jnp.float32),
        "tensor",
        scatter_dimension=0,
        tiled=True,
    )
    back_rows, back_values = (
        lax.all_to_all(
            input_part.reshape(feat_local, expert_count, capacity),
            "expert",
            split_axis=1,
            concat_axis=1,
            tiled=True,
        ),
        lax.all_to_all(
            gate_sums.reshape(1, expert_count, capacity),
            "expert",
            split_axis=1,
            concat_axis=1,
            tiled=True,
        ),
    )
    pair_inputs = lax.dot_general(
        pair_table,
        back_rows.reshape(feat_local, slot_count),
        (((0,), (1,)), ((), ())),
        precision=lax.Precision.HIGHEST,
        preferred_element_type=jnp.float32,
    )
    tokens_grad = jnp.sum(pair_inputs.reshape(token_count, top_count, feat_local), axis=1).astype(
        jnp.bfloat16
    )
    values_grad = jnp.dot(
        back_values.reshape(slot_count),
        pair_table,
        precision=lax.Precision.HIGHEST,
        preferred_element_type=jnp.float32,
    ).reshape(token_count, top_count)
    return (tokens_grad, values_grad, gate_grad[None], up_grad[None], down_grad[None])


def solution(mesh):
    in_specs = (
        P("expert", "tensor"),
        P("expert", "tensor"),
        P("expert", None),
        P("expert", None),
        P("expert", None, "tensor"),
        P("expert", None, "tensor"),
        P("expert", "tensor", None),
    )
    out_specs = (
        P("expert", "tensor"),
        P("expert", None),
        P("expert", None, "tensor"),
        P("expert", None, "tensor"),
        P("expert", "tensor", None),
    )
    return jax.shard_map(
        per_device, mesh=mesh, in_specs=in_specs, out_specs=out_specs, check_vma=False
    )
```

profile of v0, /device:TPU:1, one launch (start us, length us, event | category | flops | bytes accessed | tf_op | source)
XLA Modules:
  0.0 1034.6 jit_solution(16054552695791517856)
XLA Ops:
  7.2 0.8 copy.59
  10.3 0.8 convolution_convert_fusion.3
  11.4 14.0 %all_to_all.30 = bf16[8,2,1024]{2,1,0:T(2,128)(2,1)S(1)} all-to-all(bf16[8,2,1024]{2,1,0:T(2,128)(2,1)S(1)} %reshape.164), channel_id=1, replica_groups=mesh['expert'=8,'tensor'=64] {'expert'}, dimensions={0} | all-to-all | bytes 65536 | tf_op jit(solution)/shard_map/all_to_all | solution.py:90
  26.3 0.9 convolution_convert_fusion.4
  27.4 7.8 all_to_all.31
  36.8 7.7 all_to_all.32
  44.6 112.9 %all-gather.5.cloned.1.call-done = bf16[512,2048]{0,1:T(8,128)(2,1)} async-done(((bf16[512,32]{0,1:T(8,128)(2,1)}), bf16[512,2048]{0,1:T(8,128)(2,1)}) %all-gather.5.cloned.1.call-update) | async-done | bytes 2097168 | tf_op jit(solution)/shard_map/all_gather | solution.py:116
  157.5 2.2 fusion.6
  159.8 1.2 fusion.9
  161.0 137.0 %all-gather.3.cloned.1.call-done = bf16[512,2048]{0,1:T(8,128)(2,1)} async-done(((bf16[512,32]{0,1:T(8,128)(2,1)}), bf16[512,2048]{0,1:T(8,128)(2,1)}) %all-gather.3.cloned.1.call-update) | async-done | bytes 2097168 | tf_op jit(solution)/shard_map/all_gather | solution.py:117
  298.0 2.3 multiply_reduce_fusion
  301.0 2.7 add_bitcast_fusion
  303.8 5.3 copy.76
  309.5 113.0 %psum.7 = f32[1,8,64]{2,0,1:T(1,128)} all-reduce(f32[1,8,64]{2,0,1:T(1,128)S(1)} %reshape.137), channel_id=1, replica_groups=mesh['expert'=8,'tensor'=64] {'tensor'}, use_global_device_ids=true, to_apply=%region_7.8 | all-reduce | flops 512 | bytes 4096 | tf_op jit(solution)/shard_map/psum | solution.py:122
  422.5 43.1 %all-to-all-start.4 = ((f32[1,8,64]{2,0,1:T(1,128)}), f32[1,8,64]{2,0,1:T(1,128)S(1)}, u32[]{:S(2)}, u32[]{:S(2)}) async-start(f32[1,8,64]{2,0,1:T(1,128)} %psum.7), calls=%async_computation.4 | async-start | bytes 8192 | tf_op jit(solution)/shard_map/all_to_all | solution.py:140
  465.6 1.5 fusion
  467.2 1.6 fusion.2
  468.8 1.5 fusion.1
  471.6 531.4 %reduce-scatter.4.cloned.1.call-done = f32[32,512]{1,0:T(8,128)} async-done(((f32[2048,512]{1,0:T(8,128)}), f32[32,512]{1,0:T(8,128)}) %reduce-scatter.4.cloned.1.call-update) | async-done | bytes 65552
  1003.0 1.0 copy.77
  1004.8 15.9 %all-to-all-start.3 = ((f32[8,1,2048]{2,1,0:T(1,128)}), f32[8,1,2048]{2,1,0:T(1,128)S(1)}, u32[]{:S(2)}, u32[]{:S(2)}) async-start(f32[8,1,2048]{2,1,0:T(1,128)} %reshape.168), calls=%async_computation.3 | async-start | bytes 131072 | tf_op jit(solution)/shard_map/all_to_all | solution.py:133
  1021.8 3.8 all-to-all-done.3
  1026.1 0.8 reduce.12
  1027.1 0.9 convolution_reduce_fusion
  (70 shorter events, 10.4 us)
Async XLA Ops:
  7.2 150.3 %copy-start = (bf16[1,2048,128]{2,1,0:T(8,128)(2,1)S(1)}, bf16[1,2048,128]{2,1,0:T(8,128)(2,1)}, u32[]{:S(2)}) copy-start(bf16[1,2048,128]{2,1,0:T(8,128)(2,1)} %param.11) | copy-start | bytes 1572868
  7.2 29.0 %copy-start.7 = (bf16[128,2]{0,1:T(2,128)(2,1)S(1)}, bf16[128,2]{0,1:T(2,128)(2,1)}, u32[]{:S(2)}) copy-start(bf16[128,2]{0,1:T(2,128)(2,1)} %param.10) | copy-start | bytes 1540
  7.2 150.3 %all-gather.5.cloned.1.call-start = ((), (), s32[]{:S(2)}) async-start(), calls=%async_computation.7 | async-start | bytes 2129920 | tf_op jit(solution)/shard_map/all_gather | solution.py:116
  26.2 133.5 %copy-start.3 = (bf16[1,2048,128]{2,1,0:T(8,128)(2,1)S(1)}, bf16[1,2048,128]{2,1,0:T(8,128)(2,1)}, u32[]{:S(2)}) copy-start(bf16[1,2048,128]{2,1,0:T(8,128)(2,1)} %param.12) | copy-start | bytes 1572868
  26.2 271.8 %all-gather.3.cloned.1.call-start = ((), (), s32[]{:S(2)}) async-start(), calls=%async_computation.6 | async-start | bytes 2129920 | tf_op jit(solution)/shard_map/all_gather | solution.py:117
  36.2 966.8 %reduce-scatter.4.cloned.1.call-start = ((), (), s32[]{:S(2)}) async-start(), calls=%async_computation.8 | async-start | bytes 4259840
  157.5 2.3 copy-start.1
  300.3 0.8 copy-start.4
  309.1 156.5 %copy-start.5 = (bf16[512,128]{0,1:T(8,128)(2,1)S(1)}, bf16[512,128]{0,1:T(8,128)(2,1)}, u32[]{:S(2)}) copy-start(bf16[512,128]{0,1:T(8,128)(2,1)} %copy-done.4) | copy-start | bytes 393220
  422.5 47.8 %all-to-all-start.4 = ((f32[1,8,64]{2,0,1:T(1,128)}), f32[1,8,64]{2,0,1:T(1,128)S(1)}, u32[]{:S(2)}, u32[]{:S(2)}) async-start(f32[1,8,64]{2,0,1:T(1,128)} %psum.7), calls=%async_computation.4 | async-start | bytes 8192 | tf_op jit(solution)/shard_map/all_to_all | solution.py:140
  465.6 1.6 copy-start.2
  465.6 1.6 copy-start.6
  1004.8 20.8 %all-to-all-start.3 = ((f32[8,1,2048]{2,1,0:T(1,128)}), f32[8,1,2048]{2,1,0:T(1,128)S(1)}, u32[]{:S(2)}, u32[]{:S(2)}) async-start(f32[8,1,2048]{2,1,0:T(1,128)} %reshape.168), calls=%async_computation.3 | async-start | bytes 131072 | tf_op jit(solution)/shard_map/all_to_all | solution.py:133
Sparse Core Ops, SparseCore 0:
  26.4 131.0 all-gather.4
  161.0 136.9 all-gather.2
  309.3 693.6 reduce-scatter.3
where the time goes:
time: 1040 us; the launch traced here: 1030 us
  waiting for transfers between devices  785 us (75%)
  blocking collectives  142 us (14%)
  starting transfers between devices  59.1 us (6%)
  matrix products  16.6 us (2%)
  between operations  14 us (1%)
  local copies, waits for them, and re-layouts  13.7 us (1%)
    unnamed x4, waiting for transfers between devices  531 us
    all_gather x1, waiting for transfers between devices, per_device(): lax.all_gather(grads_in, 'tensor', axis=1, tiled=True)  137 us
    psum x1, blocking collectives, per_device(): gate_sums = lax.psum(gate_partial, 'tensor')  113 us
    all_gather x1, waiting for transfers between devices, per_device(): lax.all_gather(rows_in, 'tensor', axis=1, tiled=True)  113 us
    all_to_all x1, starting transfers between devices, per_device(): lax.all_to_all(gate_sums.reshape(1, expert_count, capacity), 'expert', sp...  43.1 us
  transfers between devices with their start and end apart: 5, of which 4 were waited for; matrix products, arithmetic and copies ran while one was open for 1% of the time, Pallas kernels for 0%

commit v1 on v0

v1 whole, which is shorter than its diff:
```python
import functools

import jax
import jax.numpy as jnp
from jax import lax
from jax.experimental import pallas as pl
from jax.experimental.pallas import tpu as pltpu
from jax.sharding import PartitionSpec as P

MESH = pl.DeviceIdType.MESH
NX = 4
contract_cols = (((1,), (1,)), ((), ()))


def cols_to_row(ref, column, count):
    rows = lax.broadcasted_iota(jnp.int32, (count, count), 0)
    cols = lax.broadcasted_iota(jnp.int32, (count, count), 1)
    values = ref[:, column : column + 1].astype(jnp.float32)
    return jnp.sum(jnp.where(rows == cols, values, 0.0), axis=0, keepdims=True)


def row_to_col(row, count):
    rows = lax.broadcasted_iota(jnp.int32, (count, count), 0)
    cols = lax.broadcasted_iota(jnp.int32, (count, count), 1)
    return jnp.sum(jnp.where(rows == cols, row, 0.0), axis=1, keepdims=True)


def kernel(
    dims,
    tok_ref, grad_ref, routes_ref, values_ref, gate_hbm, up_hbm, down_hbm,
    tgrad_ref, vgrad_ref, ggrad_hbm, ugrad_hbm, dgrad_hbm,
    xt, gt, meta, wg, wu, wd, wt, ab, hh, own, sib_out, sib_in, s1, r1a, r1b,
    s2a, s2b, s2fa, s2fb, r2a, r2b, s3, s3f, r3, vp, vr, v1, vx, vz,
    og, ou, od, stage_t, stage_g, send_sems, recv_sems, local_sems,
):
    ny, nz, feat, tokens, hidden = dims
    e = lax.axis_index("expert")
    t = lax.axis_index("tensor")
    y, c = e // 2, e % 2
    x, z = t // nz, t % nz
    slab = nz * feat
    half_slab = slab // 2
    depth = NX * slab
    groups = 2 * ny

    counter = [0]
    pending = []

    def dev(xx=None, yy=None, zz=None, cc=None):
        xx = x if xx is None else xx
        yy = y if yy is None else yy
        zz = z if zz is None else zz
        cc = c if cc is None else cc
        return (yy * 2 + cc, xx * nz + zz)

    def take(count=1):
        first = counter[0]
        counter[0] += count
        return first

    def remote(src, dst, index, device):
        return pltpu.make_async_remote_copy(
            src_ref=src, dst_ref=dst, send_sem=send_sems.at[index], recv_sem=recv_sems.at[index],
            device_id=device, device_id_type=MESH,
        )

    def send(src, dst, index, device):
        copy = remote(src, dst, index, device)
        copy.start()
        pending.append(copy)

    def arrived(ref, index):
        remote(ref, ref, index, dev()).wait_recv()

    def rem(value, size):
        return lax.rem(value + size, size)

    sibling = dev(cc=1 - c)

    loads = [
        pltpu.make_async_copy(gate_hbm.at[0], wg, local_sems.at[0]),
        pltpu.make_async_copy(up_hbm.at[0], wu, local_sems.at[1]),
        pltpu.make_async_copy(down_hbm.at[0], wd, local_sems.at[2]),
    ]
    for load in loads:
        load.start()

    barrier = pltpu.get_barrier_semaphore()
    for j in range(1, groups):
        pl.semaphore_signal(barrier, inc=1, device_id=(rem(e + j, groups), t), device_id_type=MESH)
    for j in range(1, NX):
        pl.semaphore_signal(barrier, inc=1, device_id=dev(xx=rem(x + j, NX)), device_id_type=MESH)
    for j in range(1, nz):
        pl.semaphore_signal(barrier, inc=1, device_id=dev(zz=rem(z + j, nz)), device_id_type=MESH)

    def z_rows(block):
        return pl.ds(pl.multiple_of(x * slab + block * feat, feat), feat)

    stage_t[:, :feat] = tok_ref[...].astype(jnp.float32)
    stage_g[:, :feat] = grad_ref[...].astype(jnp.float32)
    xt[c, y, z_rows(z)] = stage_t[...].T[:feat].astype(jnp.bfloat16)
    gt[c, y, z_rows(z)] = stage_g[...].T[:feat].astype(jnp.bfloat16)
    for k in range(2):
        meta[e, k : k + 1] = cols_to_row(routes_ref, k, tokens)
        meta[e, 2 + k : 3 + k] = cols_to_row(values_ref, k, tokens)

    pl.semaphore_wait(barrier, groups - 1 + NX - 1 + nz - 1)

    right, left = dev(zz=rem(z + 1, nz)), dev(zz=rem(z - 1, nz))
    n_right, n_left = nz // 2, (nz - 1) // 2
    tr, gr = take(n_right), take(n_right)
    tl, gl = take(max(n_left, 1)), take(max(n_left, 1))

    def t_block(block):
        return xt.at[c, y, z_rows(block)]

    def g_block(block):
        return gt.at[c, y, z_rows(block)]

    for s in range(n_right):
        block = rem(z - s, nz)
        if s:
            arrived(t_block(block), tr + s - 1)
        send(t_block(block), t_block(block), tr + s, right)
        if s:
            arrived(g_block(block), gr + s - 1)
        send(g_block(block), g_block(block), gr + s, right)
        if s < n_left:
            block = rem(z + s, nz)
            if s:
                arrived(t_block(block), tl + s - 1)
            send(t_block(block), t_block(block), tl + s, left)
            if s:
                arrived(g_block(block), gl + s - 1)
            send(g_block(block), g_block(block), gl + s, left)
        if s == 0:
            meta_sems = take(groups)
            for j in range(1, groups):
                send(meta.at[e], meta.at[e], meta_sems + j, (rem(e + j, groups), t))
    arrived(t_block(rem(z - n_right, nz)), tr + n_right - 1)
    arrived(g_block(rem(z - n_right, nz)), gr + n_right - 1)
    if n_left:
        arrived(t_block(rem(z + n_left, nz)), tl + n_left - 1)
        arrived(g_block(rem(z + n_left, nz)), gl + n_left - 1)

    class Ring:
        def __init__(self, me, place, block):
            self.me, self.block = me, block
            self.right, self.left = place(rem(me + 1, 4)), place(rem(me - 1, 4))
            self.base = take(6)

        def region(self, offset, half):
            return self.block(rem(self.me + offset, 4), half)

        def start(self):
            for half, way, index in ((0, self.right, 0), (1, self.left, 2), (1, self.right, 1), (0, self.left, 3)):
                send(self.region(0, half), self.region(0, half), self.base + index, way)

        def forward(self):
            arrived(self.region(-1, 0), self.base + 0)
            send(self.region(-1, 0), self.region(-1, 0), self.base + 4, self.right)
            arrived(self.region(1, 1), self.base + 2)
            send(self.region(1, 1), self.region(1, 1), self.base + 5, self.left)

        def rest(self):
            return ((-1, 1, 1), (1, 0, 3), (2, 0, 4), (2, 1, 5))

        def wait(self, item):
            offset, half, index = item
            arrived(self.region(offset, half), self.base + index)

    def x_rows(block, half=None):
        if half is None:
            return pl.ds(pl.multiple_of(block * slab, slab), slab)
        return pl.ds(pl.multiple_of(block * slab + half * half_slab, half_slab), half_slab)

    def share(region):
        index = take()
        send(region, region, index, sibling)
        return index

    t_first = Ring(x, lambda p: dev(xx=p), lambda b, h: xt.at[c, y, x_rows(b, h)])
    g_first = Ring(y, lambda p: dev(yy=p), lambda b, h: gt.at[c, b, x_rows(x, h)])
    t_first.start()
    g_first.start()
    t_first.forward()
    g_first.forward()
    for item in t_first.rest():
        t_first.wait(item)
    half_depth = depth // 2
    t_last = Ring(y, lambda p: dev(yy=p), lambda b, h: xt.at[c, b, pl.ds(h * half_depth, half_depth)])
    t_last.start()
    for item in g_first.rest():
        g_first.wait(item)
    half_y = ny // 2
    g_last = Ring(x, lambda p: dev(xx=p), lambda b, h: gt.at[c, pl.ds(h * half_y, half_y), x_rows(b)])
    g_last.start()

    shared = []

    def share_t(offset, half):
        shared.append((lambda cc, o=offset, h=half: xt.at[cc, rem(y + o, 4), pl.ds(h * half_depth, half_depth)],
                       share(t_last.region(offset, half))))

    def share_g(offset, half):
        shared.append((lambda cc, o=offset, h=half: gt.at[cc, pl.ds(h * half_y, half_y), x_rows(rem(x + o, 4))],
                       share(g_last.region(offset, half))))

    for half in range(2):
        share_t(0, half)
        share_g(0, half)

    for load in loads:
        load.wait()
    ones = (
        lax.broadcasted_iota(jnp.int32, (hidden, hidden), 0)
        == lax.broadcasted_iota(jnp.int32, (hidden, hidden), 1)
    ).astype(jnp.bfloat16)

    @pl.loop(0, NX)
    def _(i):
        rows = pl.ds(pl.multiple_of(i * slab, slab), slab)
        for k, ref in enumerate((wg, wu)):
            wt[k * hidden : (k + 1) * hidden, rows] = lax.dot_general(
                ones, ref[rows, :], contract_cols, preferred_element_type=jnp.float32
            ).astype(jnp.bfloat16)

    t_last.forward()
    g_last.forward()
    share_t(-1, 0)
    share_t(1, 1)
    share_g(-1, 0)
    share_g(1, 1)
    for item in t_last.rest():
        t_last.wait(item)
        share_t(item[0], item[1])
    for item in g_last.rest():
        g_last.wait(item)
        share_g(item[0], item[1])
    for j in range(1, groups):
        arrived(meta.at[rem(e - j, groups)], meta_sems + j)
    for region, index in shared:
        arrived(region(1 - c), index)

    @pl.loop(0, ny)
    def _(p):
        rows = jnp.concatenate([xt[0, p], xt[1, p]], axis=1)
        grads = jnp.concatenate([gt[0, p], gt[1, p]], axis=1)
        pre = jnp.dot(wt[...], rows, preferred_element_type=jnp.float32)
        hidden_grad = jnp.dot(wd[...], grads, preferred_element_type=jnp.float32)
        pre_gate, pre_up = pre[:hidden], pre[hidden:]
        info = jnp.concatenate([meta[2 * p], meta[2 * p + 1]], axis=1)
        mine = e.astype(jnp.float32)
        hit0 = (info[0:1] == mine).astype(jnp.float32)
        hit1 = (info[1:2] == mine).astype(jnp.float32)
        weight = hit0 * info[2:3] + hit1 * info[3:4]
        s = jax.nn.sigmoid(pre_gate)
        activated = pre_gate * s
        slope = s * (1.0 + pre_gate * (1.0 - s))
        gate_partial = jnp.sum(activated * pre_up * hidden_grad, axis=0, keepdims=True)
        scaled = (weight * activated * pre_up).astype(jnp.bfloat16)
        gate_pre = (weight * hidden_grad * pre_up * slope).astype(jnp.bfloat16)
        up_pre = (weight * hidden_grad * activated).astype(jnp.bfloat16)
        for k in range(2):
            lanes = slice(k * tokens, (k + 1) * tokens)
            ab[k, p, :hidden] = gate_pre[:, lanes]
            ab[k, p, hidden:] = up_pre[:, lanes]
            hh[k, p] = scaled[:, lanes]
            vp[2 * p + k, 0:1] = (gate_partial * hit0)[:, lanes]
            vp[2 * p + k, 1:2] = (gate_partial * hit1)[:, lanes]

    v_sems = take(groups)
    for j in range(1, groups):
        peer = rem(e + j, groups)
        send(vp.at[peer], vr.at[e], v_sems + j, (peer, t))

    sib_sems = take(ny)
    a_sems = take(4)
    b_sems = take(16)

    def combine(j):
        yy = rem(y + 1 + j, ny)
        arrived(sib_in.at[yy], sib_sems + j)

        @pl.loop(0, NX)
        def _(i):
            s1[yy, i] = (own[yy, i] + sib_in[yy, i].astype(jnp.float32)).astype(jnp.bfloat16)

        if j < ny - 1:
            send(s1.at[yy, :, pl.ds(0, half_slab)], r1a.at[y], a_sems + j, dev(yy=yy))
        for k in range(1, NX):
            xx = rem(x + k, NX)
            send(s1.at[yy, xx, pl.ds(half_slab, half_slab)], r1b.at[x, yy], b_sems + 4 * j + k, dev(xx=xx))

    for j in range(ny):
        yy = rem(y + 1 + j, ny)

        @pl.loop(0, NX)
        def _(i):
            rows = pl.ds(pl.multiple_of(i * slab, slab), slab)
            weights = jnp.concatenate([wg[rows, :], wu[rows, :]], axis=1)
            pair = jnp.concatenate([ab[1 - c, yy], ab[c, yy]], axis=1)
            part = jnp.dot(weights, pair, preferred_element_type=jnp.float32)
            sib_out[yy, i] = part[:, :tokens].astype(jnp.bfloat16)
            own[yy, i] = part[:, tokens:]

        send(sib_out.at[yy], sib_in.at[yy], sib_sems + j, sibling)
        if j:
            combine(j - 1)
    combine(ny - 1)

    @pl.loop(0, NX)
    def _(i):
        rows = pl.ds(pl.multiple_of(i * slab, slab), slab)
        total = jnp.zeros((slab, 2 * hidden), jnp.float32)
        for p in range(ny):
            lhs = jnp.concatenate([xt[0, p, rows, :], xt[1, p, rows, :]], axis=1)
            rhs = jnp.concatenate([ab[0, p], ab[1, p]], axis=1)
            total += lax.dot_general(lhs, rhs, contract_cols, preferred_element_type=jnp.float32)
        og[rows, :] = total[:, :hidden].astype(jnp.bfloat16)
        ou[rows, :] = total[:, hidden:].astype(jnp.bfloat16)

    for j in range(1, groups):
        arrived(vr.at[rem(e - j, groups)], v_sems + j)
    vr[e] = vp[e]
    v1[...] = sum(vr[k] for k in range(groups))
    vx_sems = take(NX)
    for k in range(1, NX):
        send(v1, vx.at[x], vx_sems + k, dev(xx=rem(x + k, NX)))

    s2a_sems, s2b_sems = take(4), take(4)
    for j in range(ny - 1):
        src = rem(y - 1 - j, ny)
        arrived(r1a.at[src], a_sems + j)
    for j in range(NX):
        xx = rem(x + 1 + j, NX)
        total = own[y, xx, :half_slab] + sib_in[y, xx, :half_slab].astype(jnp.float32)
        for k in range(1, ny):
            total += r1a[rem(y - k, ny), xx].astype(jnp.float32)
        if j < NX - 1:
            s2a[xx] = total.astype(jnp.bfloat16)
            send(s2a.at[xx], r2a.at[x], s2a_sems + j, dev(xx=xx))
        else:
            s2fa[...] = total
    for j in range(ny):
        yy = rem(y + 1 + j, ny)
        for k in range(1, NX):
            arrived(r1b.at[rem(x - k, NX), yy], b_sems + 4 * j + k)
        total = own[yy, x, half_slab:] + sib_in[yy, x, half_slab:].astype(jnp.float32)
        for k in range(1, NX):
            total += r1b[rem(x - k, NX), yy].astype(jnp.float32)
        if j < ny - 1:
            s2b[yy] = total.astype(jnp.bfloat16)
            send(s2b.at[yy], r2b.at[y], s2b_sems + j, dev(yy=yy))
        else:
            s2fb[...] = total

    @pl.loop(0, NX)
    def _(i):
        rows = pl.ds(pl.multiple_of(i * slab, slab), slab)
        total = jnp.zeros((hidden, slab), jnp.float32)
        for p in range(ny):
            lhs = jnp.concatenate([hh[0, p], hh[1, p]], axis=1)
            rhs = jnp.concatenate([gt[0, p, rows, :], gt[1, p, rows, :]], axis=1)
            total += lax.dot_general(lhs, rhs, contract_cols, preferred_element_type=jnp.float32)
        od[:, rows] = total.astype(jnp.bfloat16)

    for k in range(1, NX):
        arrived(vx.at[rem(x - k, NX)], vx_sems + k)
    vx[x] = v1[...]
    vz[z] = sum(vx[k] for k in range(NX))
    vz_sems = take(nz)
    for k in range(1, nz):
        send(vz.at[z], vz.at[z], vz_sems + k, dev(zz=rem(z + k, nz)))

    for j in range(NX - 1):
        arrived(r2a.at[rem(x - 1 - j, NX)], s2a_sems + j)
        arrived(r2b.at[rem(y - 1 - j, ny)], s2b_sems + j)
    total = s2fa[...]
    for k in range(1, NX):
        total += r2a[rem(x - k, NX)].astype(jnp.float32)
    s3f[:half_slab] = total
    s3[:half_slab] = total.astype(jnp.bfloat16)
    total = s2fb[...]
    for k in range(1, ny):
        total += r2b[rem(y - k, ny)].astype(jnp.float32)
    s3f[half_slab:] = total
    s3[half_slab:] = total.astype(jnp.bfloat16)

    s3_sems = take(nz)
    for k in range(1, nz):
        zz = rem(z + k, nz)
        rows = pl.ds(pl.multiple_of(zz * feat, feat), feat)
        send(s3.at[rows], r3.at[z], s3_sems + k, dev(zz=zz))

    stores = [
        pltpu.make_async_copy(og, ggrad_hbm.at[0], local_sems.at[3]),
        pltpu.make_async_copy(ou, ugrad_hbm.at[0], local_sems.at[4]),
        pltpu.make_async_copy(od, dgrad_hbm.at[0], local_sems.at[5]),
    ]
    for store in stores:
        store.start()

    for k in range(1, nz):
        arrived(vz.at[rem(z - k, nz)], vz_sems + k)
    sums = sum(vz[k] for k in range(nz))
    lane = lax.broadcasted_iota(jnp.int32, (tokens, 2), 1)
    vgrad_ref[...] = jnp.where(
        lane == 0, row_to_col(sums[0:1], tokens), row_to_col(sums[1:2], tokens)
    )

    for k in range(1, nz):
        arrived(r3.at[rem(z - k, nz)], s3_sems + k)
    result = s3f[pl.ds(pl.multiple_of(z * feat, feat), feat)]
    for k in range(1, nz):
        result += r3[rem(z - k, nz)].astype(jnp.float32)
    stage_t[:feat] = result
    tgrad_ref[...] = stage_t[...].T[:, :feat].astype(jnp.bfloat16)

    for store in stores:
        store.wait()
    for copy in pending:
        copy.wait_send()
    assert counter[0] <= send_sems.shape[0], counter[0]


def per_device(tokens, out_grad, routes, gate_values, gate_weight, up_weight, down_weight):
    groups = lax.axis_size("expert")
    ny, nz = groups // 2, lax.axis_size("tensor") // NX
    count, feat = tokens.shape
    depth, hidden = gate_weight.shape[1:]
    slab, half_slab = nz * feat, nz * feat // 2
    f32, bf16 = jnp.float32, jnp.bfloat16
    vmem = pl.BlockSpec(memory_space=pltpu.VMEM)
    hbm = pl.BlockSpec(memory_space=pl.ANY)
    scratch = [
        ((2, ny, depth, count), bf16),
        ((2, ny, depth, count), bf16),
        ((groups, 8, count), f32),
        ((depth, hidden), bf16),
        ((depth, hidden), bf16),
        ((hidden, depth), bf16),
        ((2 * hidden, depth), bf16),
        ((2, ny, 2 * hidden, count), bf16),
        ((2, ny, hidden, count), bf16),
        ((ny, NX, slab, count), f32),
        ((ny, NX, slab, count), bf16),
        ((ny, NX, slab, count), bf16),
        ((ny, NX, slab, count), bf16),
        ((ny, NX, half_slab, count), bf16),
        ((NX, ny, half_slab, count), bf16),
        ((NX, half_slab, count), bf16),
        ((ny, half_slab, count), bf16),
        ((half_slab, count), f32),
        ((half_slab, count), f32),
        ((NX, half_slab, count), bf16),
        ((ny, half_slab, count), bf16),
        ((slab, count), bf16),
        ((slab, count), f32),
        ((nz, feat, count), bf16),
        ((groups, 8, count), f32),
        ((groups, 8, count), f32),
        ((8, count), f32),
        ((NX, 8, count), f32),
        ((nz, 8, count), f32),
        ((depth, hidden), bf16),
        ((depth, hidden), bf16),
        ((hidden, depth), bf16),
        ((count, 128), f32),
        ((count, 128), f32),
    ]
    flops = 2 * groups * count * depth * hidden * 8
    return pl.pallas_call(
        functools.partial(kernel, (ny, nz, feat, count, hidden)),
        out_shape=(
            jax.ShapeDtypeStruct(tokens.shape, bf16),
            jax.ShapeDtypeStruct(gate_values.shape, f32),
            jax.ShapeDtypeStruct(gate_weight.shape, bf16),
            jax.ShapeDtypeStruct(up_weight.shape, bf16),
            jax.ShapeDtypeStruct(down_weight.shape, bf16),
        ),
        in_specs=[vmem] * 4 + [hbm] * 3,
        out_specs=(vmem, vmem, hbm, hbm, hbm),
        scratch_shapes=[pltpu.VMEM(shape, dtype) for shape, dtype in scratch]
        + [
            pltpu.SemaphoreType.DMA((200,)),
            pltpu.SemaphoreType.DMA((200,)),
            pltpu.SemaphoreType.DMA((6,)),
        ],
        compiler_params=pltpu.CompilerParams(
            collective_id=0, has_side_effects=True, vmem_limit_bytes=48 * 1024 * 1024
        ),
        cost_estimate=pl.CostEstimate(
            flops=flops, bytes_accessed=2**22, transcendentals=groups * count * hidden
        ),
    )(tokens, out_grad, routes, gate_values, gate_weight, up_weight, down_weight)


def solution(mesh):
    in_specs = (
        P("expert", "tensor"),
        P("expert", "tensor"),
        P("expert", None),
        P("expert", None),
        P("expert", None, "tensor"),
        P("expert", None, "tensor"),
        P("expert", "tensor", None),
    )
    out_specs = (
        P("expert", "tensor"),
        P("expert", None),
        P("expert", None, "tensor"),
        P("expert", None, "tensor"),
        P("expert", "tensor", None),
    )
    return jax.shard_map(
        per_device, mesh=mesh, in_specs=in_specs, out_specs=out_specs, check_vma=False
    )
```

time: 1040 us -> 113 us (0.11)
  the two profiles are of different devices: /device:TPU:1 before, /device:TPU:8 now
where the time goes in v1:
time: 113 us
  Pallas kernels  103 us (91%)
  local copies, waits for them, and re-layouts  9.08 us (8%)
    pallas_call x1, Pallas kernels, per_device(): pl.pallas_call(functools.partial(kernel, (ny, nz, feat, count, hidden)),...  103 us
    unnamed x19, local copies, waits for them, and re-layouts  7.76 us

profile of v1, /device:TPU:8, one launch (start us, length us, event | category | flops | bytes accessed | tf_op | source)
XLA Modules:
  0.0 113.1 jit_solution(13510713533768024900)
XLA Ops:
  0.6 0.0 copy-start.3
  0.6 0.8 copy.12.tok_ref
  1.5 0.0 copy-done.3
  1.5 0.0 copy-start.5
  1.5 0.1 copy.13.grad_ref
  1.6 0.5 copy-done.5
  2.1 0.0 copy-start.4
  2.1 0.1 copy.15.values_ref
  2.3 0.5 copy-done.4
  2.8 0.1 copy.14.routes_ref
  2.9 0.0 copy-start
  2.9 1.0 copy-done
  4.0 0.0 copy-start.1
  4.0 1.0 copy-done.1
  5.0 0.0 copy-start.2
  5.0 1.0 copy-done.2
  6.0 103.3 %shard_map.110 = (bf16[128,32]{1,0:T(8,128)(2,1)S(1)}, f32[128,2]{1,0:T(8,128)S(1)}, bf16[1,2048,128]{2,1,0:T(8,128)(2,1)S(1)}, bf16[1,2048,128]{2,1,0:T(8,128)(2,1)S(1)}, bf16[1,128,2048]{2,1,0:T(8,128)(2,1)S(1)}) custom-call(bf16[128,32]{1,0:T(8,128)(2,1)S(1)} %copy.12.tok_ref, bf16[128,32]{1,0:T(8,128)(2,1)S(1)} %copy.13.grad_ref, ...), custom_call_target="tpu_custom_call" | custom-call | flops 4294967296 | bytes 4194304 | tf_op jit(solution)/shard_map/pallas_call | solution.py:473
  109.4 0.7 copy.16
  110.1 0.6 copy.17
  110.7 0.8 copy.21
  111.5 0.8 copy.22
  112.3 0.8 copy.23
Async XLA Ops:
  0.6 0.8 copy-start.3
  1.5 0.7 copy-start.5
  2.1 0.7 copy-start.4
  2.9 1.0 copy-start
  4.0 1.0 copy-start.1
  5.0 1.0 copy-start.2

commit v2 on v0

v2 whole, which is shorter than its diff:
```python
import functools

import jax
import jax.numpy as jnp
from jax import lax
from jax.experimental import pallas as pl
from jax.experimental.pallas import tpu as pltpu
from jax.sharding import PartitionSpec as P

MESH = pl.DeviceIdType.MESH
NX = 4
DIRECT = (0, 3)
SLOT = {1: 0, 3: 1, 2: 2}
contract_cols = (((1,), (1,)), ((), ()))


def kernel(
    dims,
    tok_ref, grad_ref, routes_ref, values_ref, gate_hbm, up_hbm, down_hbm,
    tgrad_ref, vgrad_ref, ggrad_hbm, ugrad_hbm, dgrad_hbm,
    xg, meta, wg, wu, wd, wt, pre, hg, ab, hh, own, sib_out, sib_in, s1, r1a, r1b,
    s2a, s2b, s2fa, s2fb, r2a, r2b, s3, s3f, r3, vp, vr, v1, vx, vz,
    og, ou, od, send_sems, recv_sems, local_sems,
):
    ny, nz, nq, feat, tokens, hidden = dims
    e = lax.axis_index("expert")
    t = lax.axis_index("tensor")
    y, c = e // 2, e % 2
    x, z = t // nz, t % nz
    qz = nz // nq
    k, i = z // qz, z % qz
    slab = nz * feat
    quad = qz * feat
    half = quad // 2
    groups = 2 * ny
    quad_order = [0, 1, 3, 2][:nq] if nq == 4 else [0, 1]
    f32, bf16 = jnp.float32, jnp.bfloat16

    counter = [0]
    pending = []

    def rem(value, size):
        return lax.rem(value + size, size)

    def dev(xx=None, yy=None, zz=None, cc=None):
        xx = x if xx is None else xx
        yy = y if yy is None else yy
        zz = z if zz is None else zz
        cc = c if cc is None else cc
        return (yy * 2 + cc, xx * nz + zz)

    def take(count=1):
        first = counter[0]
        counter[0] += count
        return first

    def remote(src, dst, index, device):
        return pltpu.make_async_remote_copy(
            src_ref=src, dst_ref=dst, send_sem=send_sems.at[index], recv_sem=recv_sems.at[index],
            device_id=device, device_id_type=MESH,
        )

    def send(src, dst, index, device):
        copy = remote(src, dst, index, device)
        copy.start()
        pending.append(copy)

    def arrived(ref, index):
        remote(ref, ref, index, dev()).wait_recv()

    sibling = dev(cc=1 - c)

    def drain():
        for copy in pending:
            copy.wait_send()
        pending.clear()

    loads = [
        pltpu.make_async_copy(gate_hbm.at[0], wg, local_sems.at[0]),
        pltpu.make_async_copy(up_hbm.at[0], wu, local_sems.at[1]),
        pltpu.make_async_copy(down_hbm.at[0], wd, local_sems.at[2]),
    ]
    for load in loads:
        load.start()

    barrier = pltpu.get_barrier_semaphore()
    for j in range(1, groups):
        pl.semaphore_signal(barrier, inc=1, device_id=(rem(e + j, groups), t), device_id_type=MESH)
    for j in range(1, NX):
        pl.semaphore_signal(barrier, inc=1, device_id=dev(xx=rem(x + j, NX)), device_id_type=MESH)
    for j in range(1, nz):
        pl.semaphore_signal(barrier, inc=1, device_id=dev(zz=rem(z + j, nz)), device_id_type=MESH)

    def feats(block):
        return pl.ds(pl.multiple_of(block * feat, feat), feat)

    xg[0, c, y, x, feats(z)] = tok_ref[...]
    xg[1, c, y, x, feats(z)] = grad_ref[...]
    meta[e, 0:2] = routes_ref[...].astype(f32)
    meta[e, 2:4] = values_ref[...].astype(f32)
    pl.semaphore_wait(barrier, groups - 1 + NX - 1 + nz - 1)

    def z_block(block):
        return xg.at[:, c, y, x, feats(block)]

    z_sems = take(nz)

    def z_start(u):
        for s in range(1 if u == 0 else 0, qz):
            zz = rem(k + quad_order[u], nq) * qz + rem(i + s, qz)
            send(z_block(z), z_block(z), z_sems + u * qz + s, dev(zz=zz))

    z_start(0)
    meta_sems = take(groups)
    for j in range(1, groups):
        send(meta.at[e], meta.at[e], meta_sems + j, (rem(e + j, groups), t))

    for load in loads:
        load.wait()
    ones = (
        lax.broadcasted_iota(jnp.int32, (hidden, hidden), 0)
        == lax.broadcasted_iota(jnp.int32, (hidden, hidden), 1)
    ).astype(bf16)

    @pl.loop(0, NX)
    def _(n):
        rows = pl.ds(pl.multiple_of(n * slab, slab), slab)
        for m, ref in enumerate((wg, wu)):
            wt[m * hidden : (m + 1) * hidden, rows] = lax.dot_general(
                ones, ref[rows, :], contract_cols, preferred_element_type=f32
            ).astype(bf16)

    def source_quad(u):
        return rem(k - quad_order[u], nq)

    def rows_of(q):
        return pl.ds(pl.multiple_of(q * quad, quad), quad)

    first_sems = [take(6) for _ in range(nq)]
    last_sems = [take(8) for _ in range(nq)]
    share_sems = [take(10) for _ in range(nq)]
    shared = [[] for _ in range(nq)]

    def first_start(u):
        q = source_quad(u)
        for s in range(1 if u == 0 else 0, qz):
            arrived(z_block(q * qz + rem(i - s, qz)), z_sems + u * qz + s)
        for j in (1, 3, 2):
            mine = xg.at[0, c, y, x, rows_of(q)]
            send(mine, mine, first_sems[u] + j - 1, dev(xx=rem(x + j, NX)))
            mine = xg.at[1, c, y, x, rows_of(q)]
            send(mine, mine, first_sems[u] + 3 + j - 1, dev(yy=rem(y + j, ny)))

    def t_part(cc, offset, q, part=None):
        cols = pl.ds(0, NX) if part is None else pl.ds(part * (NX // 2), NX // 2)
        return xg.at[0, cc, rem(y + offset + ny, ny), cols, rows_of(q)]

    def g_part(cc, offset, q, part=None):
        cols = pl.ds(0, ny) if part is None else pl.ds(part * (ny // 2), ny // 2)
        return xg.at[1, cc, cols, rem(x + offset + NX, NX), rows_of(q)]

    def share(u, region, offset, part=None):
        q = source_quad(u)
        index = share_sems[u] + len(shared[u])
        send(region(c, offset, q, part), region(c, offset, q, part), index, sibling)
        shared[u].append((region(1 - c, offset, q, part), index))

    def last_start(u):
        q = source_quad(u)
        for j in (1, 3, 2):
            arrived(xg.at[0, c, y, rem(x - j, NX), rows_of(q)], first_sems[u] + j - 1)
        ways = (1, 3, 2) if u in DIRECT else (1, 3)
        for j in ways:
            mine = t_part(c, 0, q)
            send(mine, mine, last_sems[u] + SLOT[j], dev(yy=rem(y + j, ny)))
        for j in (1, 3, 2):
            arrived(xg.at[1, c, rem(y - j, ny), x, rows_of(q)], first_sems[u] + 3 + j - 1)
        for j in ways:
            mine = g_part(c, 0, q)
            send(mine, mine, last_sems[u] + 4 + SLOT[j], dev(xx=rem(x + j, NX)))
        share(u, t_part, 0)
        share(u, g_part, 0)

    def last_forward(u):
        if u in DIRECT:
            return
        q = source_quad(u)
        for way in (0, 1):
            step = 1 - 2 * way
            arrived(t_part(c, -step, q), last_sems[u] + way)
            part = t_part(c, -step, q, way)
            send(part, part, last_sems[u] + 2 + way, dev(yy=rem(y + step, ny)))
            arrived(g_part(c, -step, q), last_sems[u] + 4 + way)
            part = g_part(c, -step, q, way)
            send(part, part, last_sems[u] + 6 + way, dev(xx=rem(x + step, NX)))
        for step in (1, -1):
            share(u, t_part, -step)
            share(u, g_part, -step)

    def last_finish(u):
        q = source_quad(u)
        if u in DIRECT:
            for j in (1, 3, 2):
                arrived(t_part(c, -j, q), last_sems[u] + SLOT[j])
                share(u, t_part, -j)
                arrived(g_part(c, -j, q), last_sems[u] + 4 + SLOT[j])
                share(u, g_part, -j)
            return
        for way in (0, 1):
            arrived(t_part(c, 2, q, way), last_sems[u] + 2 + way)
            share(u, t_part, 2, way)
            arrived(g_part(c, 2, q, way), last_sems[u] + 6 + way)
            share(u, g_part, 2, way)

    def product(u):
        q = source_quad(u)
        for region, index in shared[u]:
            arrived(region, index)
        spans = [
            pl.ds(pl.multiple_of(n * slab + q * quad, quad), quad) for n in range(NX)
        ]

        @pl.loop(0, ny)
        def _(p):
            lhs = jnp.concatenate([wt[:, span] for span in spans], axis=1)
            rhs = jnp.concatenate(
                [
                    jnp.concatenate([xg[0, 0, p, n, rows_of(q)], xg[0, 1, p, n, rows_of(q)]], axis=1)
                    for n in range(NX)
                ],
                axis=0,
            )
            part = jnp.dot(lhs, rhs, preferred_element_type=f32)
            pre[p] = part if u == 0 else pre[p] + part
            lhs = jnp.concatenate([wd[:, span] for span in spans], axis=1)
            rhs = jnp.concatenate(
                [
                    jnp.concatenate([xg[1, 0, p, n, rows_of(q)], xg[1, 1, p, n, rows_of(q)]], axis=1)
                    for n in range(NX)
                ],
                axis=0,
            )
            part = jnp.dot(lhs, rhs, preferred_element_type=f32)
            hg[p] = part if u == 0 else hg[p] + part

    if nq == 4:
        first_start(0)
        z_start(1)
        z_start(2)
        last_start(0)
        z_start(3)
        last_forward(0)
        first_start(1)
        first_start(2)
        last_finish(0)
        last_start(1)
        last_start(2)
        first_start(3)
        product(0)
        last_forward(1)
        last_forward(2)
        last_start(3)
        last_finish(1)
        last_finish(2)
        product(1)
        product(2)
        last_forward(3)
        last_finish(3)
        product(3)
    else:
        for u in range(nq):
            if u:
                z_start(u)
            first_start(u)
            last_start(u)
            last_forward(u)
            last_finish(u)
            product(u)
    for j in range(1, groups):
        arrived(meta.at[rem(e - j, groups)], meta_sems + j)

    @pl.loop(0, ny)
    def _(p):
        pre_gate, pre_up, hidden_grad = pre[p, :hidden], pre[p, hidden:], hg[p]
        info = jnp.concatenate([meta[2 * p], meta[2 * p + 1]], axis=1)
        mine = e.astype(f32)
        hit0 = (info[0:1] == mine).astype(f32)
        hit1 = (info[1:2] == mine).astype(f32)
        weight = hit0 * info[2:3] + hit1 * info[3:4]
        s = jax.nn.sigmoid(pre_gate)
        activated = pre_gate * s
        slope = s * (1.0 + pre_gate * (1.0 - s))
        gate_partial = jnp.sum(activated * pre_up * hidden_grad, axis=0, keepdims=True)
        scaled = (weight * activated * pre_up).astype(bf16)
        gate_pre = (weight * hidden_grad * pre_up * slope).astype(bf16)
        up_pre = (weight * hidden_grad * activated).astype(bf16)
        for m in range(2):
            lanes = slice(m * tokens, (m + 1) * tokens)
            ab[m, p, :hidden] = gate_pre[:, lanes]
            ab[m, p, hidden:] = up_pre[:, lanes]
            hh[m, p] = scaled[:, lanes]
            vp[2 * p + m, 0:1] = (gate_partial * hit0)[:, lanes]
            vp[2 * p + m, 1:2] = (gate_partial * hit1)[:, lanes]

    sum_order = quad_order[::-1]
    sib_sems = take(nq)
    s1_sems = [take(6) for _ in range(nq)]
    s2_sems = [take(6) for _ in range(nq)]
    s3_sems = take(nz)

    def target_quad(u):
        return rem(k + sum_order[u], nq)

    def input_grads(u):
        q = target_quad(u)

        @pl.loop(0, ny)
        def _(p):
            spans = [
                pl.ds(pl.multiple_of(n * slab + q * quad, quad), quad) for n in range(NX)
            ]
            weights = jnp.concatenate(
                [jnp.concatenate([wg[span, :], wu[span, :]], axis=1) for span in spans], axis=0
            )
            pair = jnp.concatenate([ab[1 - c, p], ab[c, p]], axis=1)
            part = jnp.dot(weights, pair, preferred_element_type=f32)
            for n in range(NX):
                sib_out[q, p, n] = part[n * quad : (n + 1) * quad, :tokens].astype(bf16)
                own[q, p, n] = part[n * quad : (n + 1) * quad, tokens:]

        send(sib_out.at[q], sib_in.at[q], sib_sems + u, sibling)

    def first_sum(u):
        q = target_quad(u)
        arrived(sib_in.at[q], sib_sems + u)

        @pl.loop(0, ny)
        def _(p):
            s1[q, p] = (own[q, p] + sib_in[q, p].astype(f32)).astype(bf16)

        for j in (2, 1, 3):
            yy, xx = rem(y + j, ny), rem(x + j, NX)
            send(s1.at[q, yy, :, pl.ds(0, half)], r1a.at[q, y], s1_sems[u] + j - 1, dev(yy=yy))
            send(s1.at[q, :, xx, pl.ds(half, half)], r1b.at[q, x], s1_sems[u] + 3 + j - 1, dev(xx=xx))

    def second_sum(u):
        q = target_quad(u)
        for j in (1, 2, 3):
            arrived(r1a.at[q, rem(y - j, ny)], s1_sems[u] + j - 1)
        for j in (2, 1, 3, 0):
            xx = rem(x + j, NX)
            total = own[q, y, xx, :half] + sib_in[q, y, xx, :half].astype(f32)
            for m in range(1, ny):
                total += r1a[q, rem(y - m, ny), xx].astype(f32)
            if j:
                s2a[q, xx] = total.astype(bf16)
                send(s2a.at[q, xx], r2a.at[q, x], s2_sems[u] + j - 1, dev(xx=xx))
            else:
                s2fa[q] = total
        for j in (1, 2, 3):
            arrived(r1b.at[q, rem(x - j, NX)], s1_sems[u] + 3 + j - 1)
        for j in (2, 1, 3, 0):
            yy = rem(y + j, ny)
            total = own[q, yy, x, half:] + sib_in[q, yy, x, half:].astype(f32)
            for m in range(1, NX):
                total += r1b[q, rem(x - m, NX), yy].astype(f32)
            if j:
                s2b[q, yy] = total.astype(bf16)
                send(s2b.at[q, yy], r2b.at[q, y], s2_sems[u] + 3 + j - 1, dev(yy=yy))
            else:
                s2fb[q] = total

    def third_sum(u):
        q = target_quad(u)
        for j in (1, 2, 3):
            arrived(r2a.at[q, rem(x - j, NX)], s2_sems[u] + j - 1)
        total = s2fa[q]
        for m in range(1, NX):
            total += r2a[q, rem(x - m, NX)].astype(f32)
        s3f[q, :half] = total
        s3[q, :half] = total.astype(bf16)
        for j in (1, 2, 3):
            arrived(r2b.at[q, rem(y - j, ny)], s2_sems[u] + 3 + j - 1)
        total = s2fb[q]
        for m in range(1, ny):
            total += r2b[q, rem(y - m, ny)].astype(f32)
        s3f[q, half:] = total
        s3[q, half:] = total.astype(bf16)
        for s in range(1 if sum_order[u] == 0 else 0, qz):
            place = rem(i + s, qz)
            slot = u * qz + s
            send(s3.at[q, feats(place)], r3.at[slot], s3_sems + slot, dev(zz=q * qz + place))

    def gate_up_grads(n):
        rows = slice(n * slab, (n + 1) * slab)
        total = jnp.zeros((slab, 2 * hidden), f32)
        for p in range(ny):
            lhs = jnp.concatenate([xg[0, 0, p, n], xg[0, 1, p, n]], axis=1)
            rhs = jnp.concatenate([ab[0, p], ab[1, p]], axis=1)
            total += lax.dot_general(lhs, rhs, contract_cols, preferred_element_type=f32)
        og[rows, :] = total[:, :hidden].astype(bf16)
        ou[rows, :] = total[:, hidden:].astype(bf16)

    def down_grads(n):
        total = jnp.zeros((hidden, slab), f32)
        for p in range(ny):
            lhs = jnp.concatenate([hh[0, p], hh[1, p]], axis=1)
            rhs = jnp.concatenate([xg[1, 0, p, n], xg[1, 1, p, n]], axis=1)
            total += lax.dot_general(lhs, rhs, contract_cols, preferred_element_type=f32)
        od[:, n * slab : (n + 1) * slab] = total.astype(bf16)

    v_sems, vx_sems, vz_sems = take(groups), take(NX), take(nz)

    def values_start():
        for j in range(1, groups):
            peer = rem(e + j, groups)
            send(vp.at[peer], vr.at[e], v_sems + j, (peer, t))

    def values_x():
        for j in range(1, groups):
            arrived(vr.at[rem(e - j, groups)], v_sems + j)
        vr[e] = vp[e]
        v1[...] = sum(vr[m] for m in range(groups))
        for m in range(1, NX):
            send(v1, vx.at[x], vx_sems + m, dev(xx=rem(x + m, NX)))

    def values_z():
        for m in range(1, NX):
            arrived(vx.at[rem(x - m, NX)], vx_sems + m)
        vx[x] = v1[...]
        vz[z] = sum(vx[m] for m in range(NX))
        for m in range(1, nz):
            send(vz.at[z], vz.at[z], vz_sems + m, dev(zz=rem(z + m, nz)))

    stores = [
        pltpu.make_async_copy(og, ggrad_hbm.at[0], local_sems.at[3]),
        pltpu.make_async_copy(ou, ugrad_hbm.at[0], local_sems.at[4]),
        pltpu.make_async_copy(od, dgrad_hbm.at[0], local_sems.at[5]),
    ]

    for u in range(nq):
        input_grads(u)
    values_start()
    for u in range(nq):
        first_sum(u)
    values_x()
    drain()
    gate_up_grads(0)
    gate_up_grads(1)
    second_sum(0)
    gate_up_grads(2)
    gate_up_grads(3)
    stores[0].start()
    stores[1].start()
    second_sum(1)
    third_sum(0)
    values_z()
    down_grads(0)
    down_grads(1)
    for u in range(2, nq):
        second_sum(u)
        third_sum(u - 1)
        if u == 2:
            down_grads(2)
            down_grads(3)
            stores[2].start()
    if nq == 2:
        down_grads(2)
        down_grads(3)
        stores[2].start()
    third_sum(nq - 1)

    for m in range(1, nz):
        arrived(vz.at[rem(z - m, nz)], vz_sems + m)
    vgrad_ref[...] = sum(vz[m] for m in range(nz))[0:2]

    result = s3f[k, feats(i)]
    for u in range(nq):
        for s in range(1 if sum_order[u] == 0 else 0, qz):
            slot = u * qz + s
            arrived(r3.at[slot], s3_sems + slot)
            result += r3[slot].astype(f32)
    tgrad_ref[...] = result.astype(bf16)

    for store in stores:
        store.wait()

    drain()
    assert counter[0] <= send_sems.shape[0], counter[0]


def copies(count, *refs):
    sources, targets, held = refs[:count], refs[count : 2 * count], refs[2 * count : 3 * count]
    in_sems, out_sems = refs[3 * count :]
    ins = [pltpu.make_async_copy(sources[n], held[n], in_sems.at[n]) for n in range(count)]
    outs = [pltpu.make_async_copy(held[n], targets[n], out_sems.at[n]) for n in range(count)]
    for move in ins:
        move.start()
    for n in range(count):
        ins[n].wait()
        outs[n].start()
    for move in outs:
        move.wait()


def per_device(tokens, out_grad, routes, gate_values, gate_weight, up_weight, down_weight):
    groups = lax.axis_size("expert")
    ny, nz = groups // 2, lax.axis_size("tensor") // NX
    nq = 4 if nz >= 16 else 2
    count, feat = tokens.shape
    depth, hidden = gate_weight.shape[1:]
    slab, quad = nz * feat, nz // nq * feat
    half = quad // 2
    f32, bf16 = jnp.float32, jnp.bfloat16
    vmem = pl.BlockSpec(memory_space=pltpu.VMEM)
    hbm = pl.BlockSpec(memory_space=pl.ANY)
    scratch = [
        ((2, 2, ny, NX, slab, count), bf16),
        ((groups, 8, count), f32),
        ((depth, hidden), bf16),
        ((depth, hidden), bf16),
        ((hidden, depth), bf16),
        ((2 * hidden, depth), bf16),
        ((ny, 2 * hidden, 2 * count), f32),
        ((ny, hidden, 2 * count), f32),
        ((2, ny, 2 * hidden, count), bf16),
        ((2, ny, hidden, count), bf16),
        ((nq, ny, NX, quad, count), f32),
        ((nq, ny, NX, quad, count), bf16),
        ((nq, ny, NX, quad, count), bf16),
        ((nq, ny, NX, quad, count), bf16),
        ((nq, ny, NX, half, count), bf16),
        ((nq, NX, ny, half, count), bf16),
        ((nq, NX, half, count), bf16),
        ((nq, ny, half, count), bf16),
        ((nq, half, count), f32),
        ((nq, half, count), f32),
        ((nq, NX, half, count), bf16),
        ((nq, ny, half, count), bf16),
        ((nq, quad, count), bf16),
        ((nq, quad, count), f32),
        ((nz, feat, count), bf16),
        ((groups, 8, count), f32),
        ((groups, 8, count), f32),
        ((8, count), f32),
        ((NX, 8, count), f32),
        ((nz, 8, count), f32),
        ((depth, hidden), bf16),
        ((depth, hidden), bf16),
        ((hidden, depth), bf16),
    ]
    flops = 2 * groups * count * depth * hidden * 8
    out_shape = (
        jax.ShapeDtypeStruct((feat, count), bf16),
        jax.ShapeDtypeStruct((2, count), f32),
        jax.ShapeDtypeStruct(gate_weight.shape, bf16),
        jax.ShapeDtypeStruct(up_weight.shape, bf16),
        jax.ShapeDtypeStruct(down_weight.shape, bf16),
    )
    results = pl.pallas_call(
        functools.partial(kernel, (ny, nz, nq, feat, count, hidden)),
        out_shape=out_shape,
        in_specs=[vmem] * 4 + [hbm] * 3,
        out_specs=(vmem, vmem, hbm, hbm, hbm),
        scratch_shapes=[pltpu.VMEM(shape, dtype) for shape, dtype in scratch]
        + [
            pltpu.SemaphoreType.DMA((280,)),
            pltpu.SemaphoreType.DMA((280,)),
            pltpu.SemaphoreType.DMA((6,)),
        ],
        compiler_params=pltpu.CompilerParams(
            collective_id=0, has_side_effects=True, vmem_limit_bytes=60 * 1024 * 1024
        ),
        cost_estimate=pl.CostEstimate(
            flops=flops, bytes_accessed=2**22, transcendentals=groups * count * hidden
        ),
    )(tokens.T, out_grad.T, routes.T, gate_values.T, gate_weight, up_weight, down_weight)
    tokens_grad, values_grad, *weight_grads = pl.pallas_call(
        functools.partial(copies, len(results)),
        out_shape=out_shape,
        in_specs=[hbm] * len(results),
        out_specs=[hbm] * len(results),
        scratch_shapes=[pltpu.VMEM(result.shape, result.dtype) for result in results]
        + [pltpu.SemaphoreType.DMA((len(results),))] * 2,
        compiler_params=pltpu.CompilerParams(vmem_limit_bytes=60 * 1024 * 1024),
    )(*results)
    return (tokens_grad.T, values_grad.T, *weight_grads)


def solution(mesh):
    in_specs = (
        P("expert", "tensor"),
        P("expert", "tensor"),
        P("expert", None),
        P("expert", None),
        P("expert", None, "tensor"),
        P("expert", None, "tensor"),
        P("expert", "tensor", None),
    )
    out_specs = (
        P("expert", "tensor"),
        P("expert", None),
        P("expert", None, "tensor"),
        P("expert", None, "tensor"),
        P("expert", "tensor", None),
    )
    return jax.shard_map(
        per_device, mesh=mesh, in_specs=in_specs, out_specs=out_specs, check_vma=False
    )
```

time: 1040 us -> 95.8 us (0.09)
  waiting for transfers between devices: 785 us -> 0 us
  blocking collectives: 142 us -> 0 us
  Pallas kernels: 0 us -> 94.9 us
  starting transfers between devices: 59.1 us -> 0 us
  matrix products: 16.6 us -> 0 us
  local copies, waits for them, and re-layouts: 13.7 us -> 0 us
  between operations: 14 us -> 0.64 us
    unnamed x4 -> x0, waiting for transfers between devices: 531 us -> none
    all_gather x2 -> x0, waiting for transfers between devices: 250 us -> none  [the longest x1 137 us: per_device(): lax.all_gather(grads_in, 'tensor', axis=1, tiled=True)]
    psum x1 -> x0, blocking collectives: 113 us -> none  [per_device(): gate_sums = lax.psum(gate_partial, 'tensor')]
    pallas_call x0 -> x2, Pallas kernels: none -> 94.9 us  [the longest x1 92.6 us: per_device(): pl.pallas_call(functools.partial(kernel, (ny, nz, nq, feat, count, hidden...]
    all_to_all x2 -> x0, starting transfers between devices: 59 us -> none  [the longest x1 43.1 us: per_device(): lax.all_to_all(gate_sums.reshape(1, expert_count, capacity), 'expert', sp...]
    all_to_all x3 -> x0, blocking collectives: 29.4 us -> none  [the longest x1 14 us: per_device(): lax.all_to_all(rows_out.reshape(expert_count, capacity, feat_local), 'exp...]
    dot_general x12 -> x0, matrix products: 16.6 us -> none  [the longest x1 2.72 us: per_device(): lax.dot_general(up_local, up_pre_grad, contract_cols, preferred_element_t...]
  transfers between devices with their start and end apart: 5 -> 0, of which waited for: 4 -> 0; matrix products, arithmetic and copies ran while one was open for 1% -> 0% of each run, Pallas kernels for 0% -> 0%
where the time goes in v2:
time: 95.8 us; the launch traced here: 95.6 us
  Pallas kernels  94.9 us (99%)
    pallas_call x1, Pallas kernels, per_device(): pl.pallas_call(functools.partial(kernel, (ny, nz, nq, feat, count, hidden...  92.6 us
    pallas_call x1, Pallas kernels, per_device(): pl.pallas_call(functools.partial(copies, len(results)), out_shape=out_sha...  2.29 us

profile of v2, /device:TPU:1, one launch (start us, length us, event | category | flops | bytes accessed | tf_op | source)
XLA Modules:
  0.0 95.6 jit_solution(7479144267089241467)
XLA Ops:
  0.6 92.6 %shard_map.110 = (bf16[32,128]{1,0:T(8,128)(2,1)}, f32[2,128]{1,0:T(2,128)}, bf16[1,2048,128]{2,1,0:T(8,128)(2,1)}, bf16[1,2048,128]{2,1,0:T(8,128)(2,1)}, bf16[1,128,2048]{2,1,0:T(8,128)(2,1)}) custom-call(bf16[32,128]{1,0:T(8,128)(2,1)} %bitcast.6, bf16[32,128]{1,0:T(8,128)(2,1)} %bitcast.7, s32[2,128]{1,0:T(2,128)} %bitcast.9, bf16[2,128]{1,0:T(2,128)(2,1)} %bitcast.11, ...), custom_call_target="tpu_custom_call" | custom-call | flops 4294967296 | bytes 4194304 | tf_op jit(solution)/shard_map/pallas_call | solution.py:560
  93.3 2.3 %shard_map.111 = (bf16[32,128]{1,0:T(8,128)(2,1)}, f32[2,128]{1,0:T(2,128)}, bf16[1,2048,128]{2,1,0:T(8,128)(2,1)}, bf16[1,2048,128]{2,1,0:T(8,128)(2,1)}, bf16[1,128,2048]{2,1,0:T(8,128)(2,1)}) custom-call(bf16[32,128]{1,0:T(8,128)(2,1)} %get-tuple-element.15.refs_0_, f32[2,128]{1,0:T(2,128)} %get-tuple-element.16.refs_1_, ...), custom_call_target="tpu_custom_call" | custom-call | tf_op jit(solution)/shard_map/pallas_call | solution.py:578

commit v3 on v2

v3 whole, which is shorter than its diff:
```python
import functools

import jax
import jax.numpy as jnp
from jax import lax
from jax.experimental import pallas as pl
from jax.experimental.pallas import tpu as pltpu
from jax.sharding import PartitionSpec as P

MESH = pl.DeviceIdType.MESH
NX = 4
DIRECT = (0, 3)
SLOT = {1: 0, 3: 1, 2: 2}
contract_cols = (((1,), (1,)), ((), ()))


def kernel(
    dims,
    tok_ref, grad_ref, routes_ref, values_ref, gate_hbm, up_hbm, down_hbm,
    tgrad_ref, vgrad_ref, ggrad_hbm, ugrad_hbm, dgrad_hbm,
    xg, meta, wg, wu, wd, wt, pre, hg, ab, hh, own, s1, r1a, r1b,
    s2a, s2b, s2fa, s2fb, r2a, r2b, s3, s3f, r3, vp, vr, v1, vx, vz,
    og, ou, od, gu_own, gu_out, gu_in, d_own, d_out, d_in, rt, vl, send_sems, recv_sems, local_sems,
):
    ny, nz, nq, feat, tokens, hidden = dims
    e = lax.axis_index("expert")
    t = lax.axis_index("tensor")
    y, c = e // 2, e % 2
    x, z = t // nz, t % nz
    qz = nz // nq
    k, i = z // qz, z % qz
    slab = nz * feat
    quad = qz * feat
    half = quad // 2
    groups = 2 * ny
    quad_order = [0, 1, 3, 2][:nq] if nq == 4 else [0, 1]
    f32, bf16 = jnp.float32, jnp.bfloat16

    counter = [0]
    pending = []

    def rem(value, size):
        return lax.rem(value + size, size)

    def dev(xx=None, yy=None, zz=None, cc=None):
        xx = x if xx is None else xx
        yy = y if yy is None else yy
        zz = z if zz is None else zz
        cc = c if cc is None else cc
        return (yy * 2 + cc, xx * nz + zz)

    def take(count=1):
        first = counter[0]
        counter[0] += count
        return first

    def remote(src, dst, index, device):
        return pltpu.make_async_remote_copy(
            src_ref=src, dst_ref=dst, send_sem=send_sems.at[index], recv_sem=recv_sems.at[index],
            device_id=device, device_id_type=MESH,
        )

    def send(src, dst, index, device):
        copy = remote(src, dst, index, device)
        copy.start()
        pending.append(copy)

    def arrived(ref, index):
        remote(ref, ref, index, dev()).wait_recv()

    sibling = dev(cc=1 - c)

    def drain():
        for copy in pending:
            copy.wait_send()
        pending.clear()

    def feats(block):
        return pl.ds(pl.multiple_of(block * feat, feat), feat)

    inputs = [
        pltpu.make_async_copy(tok_ref, xg.at[0, y, x, feats(z)], local_sems.at[6]),
        pltpu.make_async_copy(grad_ref, xg.at[1, y, x, feats(z)], local_sems.at[7]),
        pltpu.make_async_copy(routes_ref, rt, local_sems.at[8]),
        pltpu.make_async_copy(values_ref, vl, local_sems.at[9]),
    ]
    for load in inputs:
        load.start()

    loads = [
        pltpu.make_async_copy(gate_hbm.at[0], wg.at[c], local_sems.at[0]),
        pltpu.make_async_copy(up_hbm.at[0], wu.at[c], local_sems.at[1]),
        pltpu.make_async_copy(down_hbm.at[0], wd.at[c], local_sems.at[2]),
    ]
    for load in loads:
        load.start()

    barrier = pltpu.get_barrier_semaphore()
    for j in range(nz // 2, 0, -1):
        for zz in sorted({j, nz - j}):
            pl.semaphore_signal(barrier, inc=1, device_id=dev(zz=rem(z + zz, nz)), device_id_type=MESH)
    for j in range(1, NX):
        pl.semaphore_signal(barrier, inc=1, device_id=dev(xx=rem(x + j, NX)), device_id_type=MESH)
    for j in range(1, ny):
        pl.semaphore_signal(barrier, inc=1, device_id=dev(yy=rem(y + j, ny)), device_id_type=MESH)
    pl.semaphore_signal(barrier, inc=1, device_id=sibling, device_id_type=MESH)

    for load in inputs:
        load.wait()
    meta[y, 0:2] = rt[...].astype(f32)
    meta[y, 2:4] = vl[...].astype(f32)
    pl.semaphore_wait(barrier, ny - 1 + NX - 1 + nz - 1 + 1)

    def z_block(block):
        return xg.at[:, y, x, feats(block)]

    z_sems = take(nz)

    def z_start(u):
        for s in range(1 if u == 0 else 0, qz):
            zz = rem(k + quad_order[u], nq) * qz + rem(i + s, qz)
            send(z_block(z), z_block(z), z_sems + u * qz + s, dev(zz=zz))

    z_start(0)
    meta_sems = take(ny)
    for j in range(1, ny):
        send(meta.at[y], meta.at[y], meta_sems + j, dev(yy=rem(y + j, ny)))

    for load in loads:
        load.wait()
    w_sems = take(3)
    for n, ref in enumerate((wg, wu, wd)):
        send(ref.at[c], ref.at[c], w_sems + n, sibling)
    ones = (
        lax.broadcasted_iota(jnp.int32, (hidden, hidden), 0)
        == lax.broadcasted_iota(jnp.int32, (hidden, hidden), 1)
    ).astype(bf16)

    def transpose(core):
        @pl.loop(0, NX)
        def _(n):
            rows = pl.ds(pl.multiple_of(n * slab, slab), slab)
            for m, ref in enumerate((wg, wu)):
                places = pl.ds(pl.multiple_of((2 * core + m) * hidden, hidden), hidden)
                wt[places, rows] = lax.dot_general(
                    ones, ref[core, rows, :], contract_cols, preferred_element_type=f32
                ).astype(bf16)

    transpose(c)

    def transpose_sibling():
        for n, ref in enumerate((wg, wu, wd)):
            arrived(ref.at[1 - c], w_sems + n)
        transpose(1 - c)

    def source_quad(u):
        return rem(k - quad_order[u], nq)

    def rows_of(q):
        return pl.ds(pl.multiple_of(q * quad, quad), quad)

    first_sems = [take(6) for _ in range(nq)]
    last_sems = [take(8) for _ in range(nq)]

    def first_start(u):
        q = source_quad(u)
        for s in range(1 if u == 0 else 0, qz):
            arrived(z_block(q * qz + rem(i - s, qz)), z_sems + u * qz + s)
        for j in (1, 3, 2):
            mine = xg.at[0, y, x, rows_of(q)]
            send(mine, mine, first_sems[u] + j - 1, dev(xx=rem(x + j, NX)))
            mine = xg.at[1, y, x, rows_of(q)]
            send(mine, mine, first_sems[u] + 3 + j - 1, dev(yy=rem(y + j, ny)))

    def t_part(offset, q, part=None):
        cols = pl.ds(0, NX) if part is None else pl.ds(part * (NX // 2), NX // 2)
        return xg.at[0, rem(y + offset + ny, ny), cols, rows_of(q)]

    def g_part(offset, q, part=None):
        cols = pl.ds(0, ny) if part is None else pl.ds(part * (ny // 2), ny // 2)
        return xg.at[1, cols, rem(x + offset + NX, NX), rows_of(q)]

    def last_start(u):
        q = source_quad(u)
        for j in (1, 3, 2):
            arrived(xg.at[0, y, rem(x - j, NX), rows_of(q)], first_sems[u] + j - 1)
        ways = (1, 3, 2) if u in DIRECT else (1, 3)
        for j in ways:
            mine = t_part(0, q)
            send(mine, mine, last_sems[u] + SLOT[j], dev(yy=rem(y + j, ny)))
        for j in (1, 3, 2):
            arrived(xg.at[1, rem(y - j, ny), x, rows_of(q)], first_sems[u] + 3 + j - 1)
        for j in ways:
            mine = g_part(0, q)
            send(mine, mine, last_sems[u] + 4 + SLOT[j], dev(xx=rem(x + j, NX)))

    def last_forward(u):
        if u in DIRECT:
            return
        q = source_quad(u)
        for way in (0, 1):
            step = 1 - 2 * way
            arrived(t_part(-step, q), last_sems[u] + way)
            part = t_part(-step, q, way)
            send(part, part, last_sems[u] + 2 + way, dev(yy=rem(y + step, ny)))
            arrived(g_part(-step, q), last_sems[u] + 4 + way)
            part = g_part(-step, q, way)
            send(part, part, last_sems[u] + 6 + way, dev(xx=rem(x + step, NX)))

    def last_finish(u):
        q = source_quad(u)
        if u in DIRECT:
            for j in (1, 3, 2):
                arrived(t_part(-j, q), last_sems[u] + SLOT[j])
                arrived(g_part(-j, q), last_sems[u] + 4 + SLOT[j])
            return
        for way in (0, 1):
            arrived(t_part(2, q, way), last_sems[u] + 2 + way)
            arrived(g_part(2, q, way), last_sems[u] + 6 + way)

    def product(u):
        q = source_quad(u)
        spans = [
            pl.ds(pl.multiple_of(n * slab + q * quad, quad), quad) for n in range(NX)
        ]

        @pl.loop(0, ny // 2)
        def _(p):
            def rhs(kind):
                return jnp.concatenate(
                    [
                        jnp.concatenate(
                            [xg[kind, 2 * p, n, rows_of(q)], xg[kind, 2 * p + 1, n, rows_of(q)]], axis=1
                        )
                        for n in range(NX)
                    ],
                    axis=0,
                )

            lhs = jnp.concatenate([wt[:, span] for span in spans], axis=1)
            part = jnp.dot(lhs, rhs(0), preferred_element_type=f32)
            pre[p] = part if u == 0 else pre[p] + part
            lhs = jnp.concatenate(
                [jnp.concatenate([wd[m, :, span] for span in spans], axis=1) for m in range(2)], axis=0
            )
            part = jnp.dot(lhs, rhs(1), preferred_element_type=f32)
            hg[p] = part if u == 0 else hg[p] + part

    if nq == 4:
        first_start(0)
        z_start(1)
        z_start(2)
        last_start(0)
        transpose_sibling()
        last_forward(0)
        first_start(1)
        z_start(3)
        first_start(2)
        last_finish(0)
        last_start(1)
        last_start(2)
        first_start(3)
        product(0)
        last_forward(1)
        last_forward(2)
        last_start(3)
        last_finish(1)
        last_finish(2)
        product(1)
        product(2)
        last_forward(3)
        last_finish(3)
        product(3)
    else:
        for u in range(nq):
            if u:
                z_start(u)
            else:
                transpose_sibling()
            first_start(u)
            last_start(u)
            last_forward(u)
            last_finish(u)
            product(u)
    for j in range(1, ny):
        arrived(meta.at[rem(y - j, ny)], meta_sems + j)

    @pl.loop(0, ny // 2)
    def _(p):
        info = jnp.concatenate([meta[2 * p], meta[2 * p + 1]], axis=1)
        sums = [0.0, 0.0]
        for m in range(2):
            rows = 2 * m * hidden
            pre_gate, pre_up = pre[p, rows : rows + hidden], pre[p, rows + hidden : rows + 2 * hidden]
            hidden_grad = hg[p, m * hidden : (m + 1) * hidden]
            mine = (y * 2 + m).astype(f32)
            hit0 = (info[0:1] == mine).astype(f32)
            hit1 = (info[1:2] == mine).astype(f32)
            weight = hit0 * info[2:3] + hit1 * info[3:4]
            s = jax.nn.sigmoid(pre_gate)
            activated = pre_gate * s
            slope = s * (1.0 + pre_gate * (1.0 - s))
            gate_partial = jnp.sum(activated * pre_up * hidden_grad, axis=0, keepdims=True)
            scaled = (weight * activated * pre_up).astype(bf16)
            gate_pre = (weight * hidden_grad * pre_up * slope).astype(bf16)
            up_pre = (weight * hidden_grad * activated).astype(bf16)
            sums[0] += gate_partial * hit0
            sums[1] += gate_partial * hit1
            for n in range(2):
                lanes = slice(n * tokens, (n + 1) * tokens)
                ab[m, 2 * p + n, :hidden] = gate_pre[:, lanes]
                ab[m, 2 * p + n, hidden:] = up_pre[:, lanes]
                hh[m, 2 * p + n] = scaled[:, lanes]
        for n in range(2):
            lanes = slice(n * tokens, (n + 1) * tokens)
            vp[2 * p + n, 0:1] = sums[0][:, lanes]
            vp[2 * p + n, 1:2] = sums[1][:, lanes]

    sum_order = quad_order[::-1]
    s1_sems = [take(6) for _ in range(nq)]
    s2_sems = [take(6) for _ in range(nq)]
    s3_sems = take(nz)

    def target_quad(u):
        return rem(k + sum_order[u], nq)

    def input_grads(u):
        q = target_quad(u)

        @pl.loop(0, ny // 2)
        def _(p):
            spans = [
                pl.ds(pl.multiple_of(n * slab + q * quad, quad), quad) for n in range(NX)
            ]
            weights = jnp.concatenate(
                [
                    jnp.concatenate([wg[0, span], wu[0, span], wg[1, span], wu[1, span]], axis=1)
                    for span in spans
                ],
                axis=0,
            )
            pair = jnp.concatenate(
                [jnp.concatenate([ab[m, 2 * p], ab[m, 2 * p + 1]], axis=1) for m in range(2)], axis=0
            )
            part = jnp.dot(weights, pair, preferred_element_type=f32)
            for n in range(NX):
                for m in range(2):
                    piece = part[n * quad : (n + 1) * quad, m * tokens : (m + 1) * tokens]
                    own[q, 2 * p + m, n] = piece
                    s1[q, 2 * p + m, n] = piece.astype(bf16)

    def first_sum(u):
        q = target_quad(u)
        for j in (2, 1, 3):
            yy, xx = rem(y + j, ny), rem(x + j, NX)
            send(s1.at[q, yy, :, pl.ds(0, half)], r1a.at[q, y], s1_sems[u] + j - 1, dev(yy=yy))
            send(s1.at[q, :, xx, pl.ds(half, half)], r1b.at[q, x], s1_sems[u] + 3 + j - 1, dev(xx=xx))

    def second_sum(u):
        q = target_quad(u)
        for j in (1, 2, 3):
            arrived(r1a.at[q, rem(y - j, ny)], s1_sems[u] + j - 1)
        for j in (2, 1, 3, 0):
            xx = rem(x + j, NX)
            total = own[q, y, xx, :half]
            for m in range(1, ny):
                total += r1a[q, rem(y - m, ny), xx].astype(f32)
            if j:
                s2a[q, xx] = total.astype(bf16)
                send(s2a.at[q, xx], r2a.at[q, x], s2_sems[u] + j - 1, dev(xx=xx))
            else:
                s2fa[q] = total
        for j in (1, 2, 3):
            arrived(r1b.at[q, rem(x - j, NX)], s1_sems[u] + 3 + j - 1)
        for j in (2, 1, 3, 0):
            yy = rem(y + j, ny)
            total = own[q, yy, x, half:]
            for m in range(1, NX):
                total += r1b[q, rem(x - m, NX), yy].astype(f32)
            if j:
                s2b[q, yy] = total.astype(bf16)
                send(s2b.at[q, yy], r2b.at[q, y], s2_sems[u] + 3 + j - 1, dev(yy=yy))
            else:
                s2fb[q] = total

    def third_sum(u):
        q = target_quad(u)
        for j in (1, 2, 3):
            arrived(r2a.at[q, rem(x - j, NX)], s2_sems[u] + j - 1)
        total = s2fa[q]
        for m in range(1, NX):
            total += r2a[q, rem(x - m, NX)].astype(f32)
        s3f[q, :half] = total
        s3[q, :half] = total.astype(bf16)
        for j in (1, 2, 3):
            arrived(r2b.at[q, rem(y - j, ny)], s2_sems[u] + 3 + j - 1)
        total = s2fb[q]
        for m in range(1, ny):
            total += r2b[q, rem(y - m, ny)].astype(f32)
        s3f[q, half:] = total
        s3[q, half:] = total.astype(bf16)
        for s in range(1 if sum_order[u] == 0 else 0, qz):
            place = rem(i + s, qz)
            slot = u * qz + s
            send(s3.at[q, feats(place)], r3.at[slot], s3_sems + slot, dev(zz=q * qz + place))

    gu_sems, d_sems = take(2), take(2)

    def both(ref, core, p):
        return jnp.concatenate([ref[core, 2 * p], ref[core, 2 * p + 1]], axis=1)

    def gate_up_grads(first, last):
        @pl.loop(first, last)
        def _(n):
            total = jnp.zeros((slab, 4 * hidden), f32)
            for p in range(ny // 2):
                lhs = jnp.concatenate([xg[0, 2 * p, n], xg[0, 2 * p + 1, n]], axis=1)
                rhs = jnp.concatenate([both(ab, c, p), both(ab, 1 - c, p)], axis=0)
                total += lax.dot_general(lhs, rhs, contract_cols, preferred_element_type=f32)
            gu_own[n] = total[:, : 2 * hidden]
            gu_out[n] = total[:, 2 * hidden :]

        part = pl.ds(first, last - first)
        send(gu_out.at[part], gu_in.at[part], gu_sems + (1 if first else 0), sibling)

    def down_grads(first, last):
        @pl.loop(first, last)
        def _(n):
            total = jnp.zeros((2 * hidden, slab), f32)
            for p in range(ny // 2):
                lhs = jnp.concatenate([both(hh, c, p), both(hh, 1 - c, p)], axis=0)
                rhs = jnp.concatenate([xg[1, 2 * p, n], xg[1, 2 * p + 1, n]], axis=1)
                total += lax.dot_general(lhs, rhs, contract_cols, preferred_element_type=f32)
            d_own[n] = total[:hidden]
            d_out[n] = total[hidden:]

        part = pl.ds(first, last - first)
        send(d_out.at[part], d_in.at[part], d_sems + (1 if first else 0), sibling)

    def finish_gate_up(first, last):
        arrived(gu_in.at[pl.ds(first, last - first)], gu_sems + (1 if first else 0))

        @pl.loop(first, last)
        def _(n):
            rows = pl.ds(pl.multiple_of(n * slab, slab), slab)
            total = gu_own[n] + gu_in[n]
            og[rows, :] = total[:, :hidden].astype(bf16)
            ou[rows, :] = total[:, hidden:].astype(bf16)

        if last == NX:
            stores[0].start()
            stores[1].start()

    def finish_down(first, last):
        arrived(d_in.at[pl.ds(first, last - first)], d_sems + (1 if first else 0))

        @pl.loop(first, last)
        def _(n):
            rows = pl.ds(pl.multiple_of(n * slab, slab), slab)
            od[:, rows] = (d_own[n] + d_in[n]).astype(bf16)

        if last == NX:
            stores[2].start()

    v_sems, vx_sems, vz_sems = take(ny), take(NX), take(nz)

    def values_start():
        for j in range(1, ny):
            yy = rem(y + j, ny)
            send(vp.at[yy], vr.at[y], v_sems + j, dev(yy=yy))

    def values_x():
        for j in range(1, ny):
            arrived(vr.at[rem(y - j, ny)], v_sems + j)
        vr[y] = vp[y]
        v1[...] = sum(vr[m] for m in range(ny))
        for m in range(1, NX):
            send(v1, vx.at[x], vx_sems + m, dev(xx=rem(x + m, NX)))

    def values_z():
        for m in range(1, NX):
            arrived(vx.at[rem(x - m, NX)], vx_sems + m)
        vx[x] = v1[...]
        vz[z] = sum(vx[m] for m in range(NX))
        for m in range(1, nz):
            send(vz.at[z], vz.at[z], vz_sems + m, dev(zz=rem(z + m, nz)))

    stores = [
        pltpu.make_async_copy(og, ggrad_hbm.at[0], local_sems.at[3]),
        pltpu.make_async_copy(ou, ugrad_hbm.at[0], local_sems.at[4]),
        pltpu.make_async_copy(od, dgrad_hbm.at[0], local_sems.at[5]),
    ]

    if nq == 4:
        input_grads(0)
        first_sum(0)
        values_start()
        input_grads(1)
        first_sum(1)
        input_grads(2)
        input_grads(3)
        first_sum(2)
        values_x()
        drain()
        second_sum(0)
        first_sum(3)
        gate_up_grads(0, NX // 2)
        second_sum(1)
        third_sum(0)
        gate_up_grads(NX // 2, NX)
        values_z()
        second_sum(2)
        third_sum(1)
        down_grads(0, NX // 2)
        finish_gate_up(0, NX // 2)
        finish_gate_up(NX // 2, NX)
        second_sum(3)
        third_sum(2)
        down_grads(NX // 2, NX)
        finish_down(0, NX // 2)
        finish_down(NX // 2, NX)
        third_sum(3)
    else:
        for u in range(nq):
            input_grads(u)
        values_start()
        for u in range(nq):
            first_sum(u)
        values_x()
        gate_up_grads(0, NX // 2)
        gate_up_grads(NX // 2, NX)
        for u in range(nq):
            second_sum(u)
        values_z()
        down_grads(0, NX // 2)
        down_grads(NX // 2, NX)
        finish_gate_up(0, NX // 2)
        finish_gate_up(NX // 2, NX)
        finish_down(0, NX // 2)
        finish_down(NX // 2, NX)
        for u in range(nq):
            third_sum(u)
    drain()

    for m in range(1, nz):
        arrived(vz.at[rem(z - m, nz)], vz_sems + m)
    vgrad_ref[...] = sum(vz[m] for m in range(nz))[0:2]

    result = s3f[k, feats(i)]
    for u in range(nq):
        for s in range(1 if sum_order[u] == 0 else 0, qz):
            slot = u * qz + s
            arrived(r3.at[slot], s3_sems + slot)
            result += r3[slot].astype(f32)
    tgrad_ref[...] = result.astype(bf16)

    for store in stores:
        store.wait()

    drain()
    assert counter[0] <= send_sems.shape[0], counter[0]


def copies(count, *refs):
    sources, targets, held = refs[:count], refs[count : 2 * count], refs[2 * count : 3 * count]
    in_sems, out_sems = refs[3 * count :]
    ins = [pltpu.make_async_copy(sources[n], held[n], in_sems.at[n]) for n in range(count)]
    outs = [pltpu.make_async_copy(held[n], targets[n], out_sems.at[n]) for n in range(count)]
    for move in ins:
        move.start()
    for n in range(count):
        ins[n].wait()
        outs[n].start()
    for move in outs:
        move.wait()


def per_device(tokens, out_grad, routes, gate_values, gate_weight, up_weight, down_weight):
    groups = lax.axis_size("expert")
    ny, nz = groups // 2, lax.axis_size("tensor") // NX
    nq = 4 if nz >= 16 else 2
    count, feat = tokens.shape
    depth, hidden = gate_weight.shape[1:]
    slab, quad = nz * feat, nz // nq * feat
    half = quad // 2
    f32, bf16 = jnp.float32, jnp.bfloat16
    vmem = pl.BlockSpec(memory_space=pltpu.VMEM)
    hbm = pl.BlockSpec(memory_space=pl.ANY)
    scratch = [
        ((2, ny, NX, slab, count), bf16),
        ((ny, 8, count), f32),
        ((2, depth, hidden), bf16),
        ((2, depth, hidden), bf16),
        ((2, hidden, depth), bf16),
        ((4 * hidden, depth), bf16),
        ((ny // 2, 4 * hidden, 2 * count), f32),
        ((ny // 2, 2 * hidden, 2 * count), f32),
        ((2, ny, 2 * hidden, count), bf16),
        ((2, ny, hidden, count), bf16),
        ((nq, ny, NX, quad, count), f32),
        ((nq, ny, NX, quad, count), bf16),
        ((nq, ny, NX, half, count), bf16),
        ((nq, NX, ny, half, count), bf16),
        ((nq, NX, half, count), bf16),
        ((nq, ny, half, count), bf16),
        ((nq, half, count), f32),
        ((nq, half, count), f32),
        ((nq, NX, half, count), bf16),
        ((nq, ny, half, count), bf16),
        ((nq, quad, count), bf16),
        ((nq, quad, count), f32),
        ((nz, feat, count), bf16),
        ((ny, 8, count), f32),
        ((ny, 8, count), f32),
        ((8, count), f32),
        ((NX, 8, count), f32),
        ((nz, 8, count), f32),
        ((depth, hidden), bf16),
        ((depth, hidden), bf16),
        ((hidden, depth), bf16),
        ((NX, slab, 2 * hidden), f32),
        ((NX, slab, 2 * hidden), f32),
        ((NX, slab, 2 * hidden), f32),
        ((NX, hidden, slab), f32),
        ((NX, hidden, slab), f32),
        ((NX, hidden, slab), f32),
        ((2, count), jnp.int32),
        ((2, count), bf16),
    ]
    flops = 2 * groups * count * depth * hidden * 8
    out_shape = (
        jax.ShapeDtypeStruct((feat, count), bf16),
        jax.ShapeDtypeStruct((2, count), f32),
        jax.ShapeDtypeStruct(gate_weight.shape, bf16),
        jax.ShapeDtypeStruct(up_weight.shape, bf16),
        jax.ShapeDtypeStruct(down_weight.shape, bf16),
    )
    results = pl.pallas_call(
        functools.partial(kernel, (ny, nz, nq, feat, count, hidden)),
        out_shape=out_shape,
        in_specs=[hbm] * 7,
        out_specs=(vmem, vmem, hbm, hbm, hbm),
        scratch_shapes=[pltpu.VMEM(shape, dtype) for shape, dtype in scratch]
        + [
            pltpu.SemaphoreType.DMA((280,)),
            pltpu.SemaphoreType.DMA((280,)),
            pltpu.SemaphoreType.DMA((10,)),
        ],
        compiler_params=pltpu.CompilerParams(
            collective_id=0, has_side_effects=True, vmem_limit_bytes=60 * 1024 * 1024
        ),
        cost_estimate=pl.CostEstimate(
            flops=flops, bytes_accessed=2**22, transcendentals=groups * count * hidden
        ),
    )(tokens.T, out_grad.T, routes.T, gate_values.T, gate_weight, up_weight, down_weight)
    tokens_grad, values_grad, *weight_grads = pl.pallas_call(
        functools.partial(copies, len(results)),
        out_shape=out_shape,
        in_specs=[hbm] * len(results),
        out_specs=[hbm] * len(results),
        scratch_shapes=[pltpu.VMEM(result.shape, result.dtype) for result in results]
        + [pltpu.SemaphoreType.DMA((len(results),))] * 2,
        compiler_params=pltpu.CompilerParams(vmem_limit_bytes=60 * 1024 * 1024),
    )(*results)
    return (tokens_grad.T, values_grad.T, *weight_grads)


def solution(mesh):
    in_specs = (
        P("expert", "tensor"),
        P("expert", "tensor"),
        P("expert", None),
        P("expert", None),
        P("expert", None, "tensor"),
        P("expert", None, "tensor"),
        P("expert", "tensor", None),
    )
    out_specs = (
        P("expert", "tensor"),
        P("expert", None),
        P("expert", None, "tensor"),
        P("expert", None, "tensor"),
        P("expert", "tensor", None),
    )
    return jax.shard_map(
        per_device, mesh=mesh, in_specs=in_specs, out_specs=out_specs, check_vma=False
    )
```

time: 95.8 us -> 84.6 us (0.88)
  Pallas kernels: 94.9 us -> 83.7 us
    pallas_call x1, Pallas kernels: 92.6 us -> 81.5 us  [per_device(): pl.pallas_call(functools.partial(kernel, (ny, nz, nq, feat, count, hidden...]
where the time goes in v3:
time: 84.6 us; the launch traced here: 84.4 us
  Pallas kernels  83.7 us (99%)
    pallas_call x1, Pallas kernels, per_device(): pl.pallas_call(functools.partial(kernel, (ny, nz, nq, feat, count, hidden...  81.5 us
    pallas_call x1, Pallas kernels, per_device(): pl.pallas_call(functools.partial(copies, len(results)), out_shape=out_sha...  2.29 us

profile of v3, /device:TPU:1, one launch (start us, length us, event | category | flops | bytes accessed | tf_op | source)
XLA Modules:
  0.0 84.4 jit_solution(12473571314864854256)
XLA Ops:
  0.6 81.5 %shard_map.110 = (bf16[32,128]{1,0:T(8,128)(2,1)}, f32[2,128]{1,0:T(2,128)}, bf16[1,2048,128]{2,1,0:T(8,128)(2,1)}, bf16[1,2048,128]{2,1,0:T(8,128)(2,1)}, bf16[1,128,2048]{2,1,0:T(8,128)(2,1)}) custom-call(bf16[32,128]{1,0:T(8,128)(2,1)} %bitcast.6, bf16[32,128]{1,0:T(8,128)(2,1)} %bitcast.7, s32[2,128]{1,0:T(2,128)} %bitcast.9, bf16[2,128]{1,0:T(2,128)(2,1)} %bitcast.11, ...), custom_call_target="tpu_custom_call" | custom-call | flops 4294967296 | bytes 4194304 | tf_op jit(solution)/shard_map/pallas_call | solution.py:638
  82.1 2.3 %shard_map.111 = (bf16[32,128]{1,0:T(8,128)(2,1)}, f32[2,128]{1,0:T(2,128)}, bf16[1,2048,128]{2,1,0:T(8,128)(2,1)}, bf16[1,2048,128]{2,1,0:T(8,128)(2,1)}, bf16[1,128,2048]{2,1,0:T(8,128)(2,1)}) custom-call(bf16[32,128]{1,0:T(8,128)(2,1)} %get-tuple-element.15.refs_0_, f32[2,128]{1,0:T(2,128)} %get-tuple-element.16.refs_1_, ...), custom_call_target="tpu_custom_call" | custom-call | tf_op jit(solution)/shard_map/pallas_call | solution.py:656

commit v4 on v3

--- a/solution.py
+++ b/solution.py
@@ -252,14 +252,14 @@
         z_start(2)
         last_start(0)
         transpose_sibling()
-        last_forward(0)
         first_start(1)
         z_start(3)
         first_start(2)
-        last_finish(0)
+        last_forward(0)
         last_start(1)
         last_start(2)
         first_start(3)
+        last_finish(0)
         product(0)
         last_forward(1)
         last_forward(2)

time: 84.6 us -> 84.6 us (level)
  no operation moved by 1% of the time
where the time goes in v4:
time: 84.6 us; the launch traced here: 84.4 us
  Pallas kernels  83.7 us (99%)
    pallas_call x1, Pallas kernels, per_device(): pl.pallas_call(functools.partial(kernel, (ny, nz, nq, feat, count, hidden...  81.5 us
    pallas_call x1, Pallas kernels, per_device(): pl.pallas_call(functools.partial(copies, len(results)), out_shape=out_sha...  2.29 us

profile of v4, /device:TPU:1, one launch (start us, length us, event | category | flops | bytes accessed | tf_op | source)
XLA Modules:
  0.0 84.4 jit_solution(8102400664531564245)
XLA Ops:
  0.6 81.5 %shard_map.110 = (bf16[32,128]{1,0:T(8,128)(2,1)}, f32[2,128]{1,0:T(2,128)}, bf16[1,2048,128]{2,1,0:T(8,128)(2,1)}, bf16[1,2048,128]{2,1,0:T(8,128)(2,1)}, bf16[1,128,2048]{2,1,0:T(8,128)(2,1)}) custom-call(bf16[32,128]{1,0:T(8,128)(2,1)} %bitcast.6, bf16[32,128]{1,0:T(8,128)(2,1)} %bitcast.7, s32[2,128]{1,0:T(2,128)} %bitcast.9, bf16[2,128]{1,0:T(2,128)(2,1)} %bitcast.11, ...), custom_call_target="tpu_custom_call" | custom-call | flops 4294967296 | bytes 4194304 | tf_op jit(solution)/shard_map/pallas_call | solution.py:638
  82.1 2.3 %shard_map.111 = (bf16[32,128]{1,0:T(8,128)(2,1)}, f32[2,128]{1,0:T(2,128)}, bf16[1,2048,128]{2,1,0:T(8,128)(2,1)}, bf16[1,2048,128]{2,1,0:T(8,128)(2,1)}, bf16[1,128,2048]{2,1,0:T(8,128)(2,1)}) custom-call(bf16[32,128]{1,0:T(8,128)(2,1)} %get-tuple-element.15.refs_0_, f32[2,128]{1,0:T(2,128)} %get-tuple-element.16.refs_1_, ...), custom_call_target="tpu_custom_call" | custom-call | tf_op jit(solution)/shard_map/pallas_call | solution.py:656

commit v5 on v4

--- a/solution.py
+++ b/solution.py
@@ -346,8 +346,15 @@
             for n in range(NX):
                 for m in range(2):
                     piece = part[n * quad : (n + 1) * quad, m * tokens : (m + 1) * tokens]
-                    own[q, 2 * p + m, n] = piece
                     s1[q, 2 * p + m, n] = piece.astype(bf16)
+
+                    @pl.when(2 * p + m == y)
+                    def _():
+                        own[q, 2 * p + m, n, :half] = piece[:half]
+
+                    @pl.when(x == n)
+                    def _():
+                        own[q, 2 * p + m, n, half:] = piece[half:]
 
     def first_sum(u):
         q = target_quad(u)

time: 84.6 us -> 84.8 us (level)
  no operation moved by 1% of the time
where the time goes in v5:
time: 84.8 us; the launch traced here: 84.6 us
  Pallas kernels  83.9 us (99%)
    pallas_call x1, Pallas kernels, per_device(): pl.pallas_call(functools.partial(kernel, (ny, nz, nq, feat, count, hidden...  81.6 us
    pallas_call x1, Pallas kernels, per_device(): pl.pallas_call(functools.partial(copies, len(results)), out_shape=out_sha...  2.29 us

profile of v5, /device:TPU:1, one launch (start us, length us, event | category | flops | bytes accessed | tf_op | source)
XLA Modules:
  0.0 84.6 jit_solution(9089844200009268546)
XLA Ops:
  0.6 81.6 %shard_map.110 = (bf16[32,128]{1,0:T(8,128)(2,1)}, f32[2,128]{1,0:T(2,128)}, bf16[1,2048,128]{2,1,0:T(8,128)(2,1)}, bf16[1,2048,128]{2,1,0:T(8,128)(2,1)}, bf16[1,128,2048]{2,1,0:T(8,128)(2,1)}) custom-call(bf16[32,128]{1,0:T(8,128)(2,1)} %bitcast.6, bf16[32,128]{1,0:T(8,128)(2,1)} %bitcast.7, s32[2,128]{1,0:T(2,128)} %bitcast.9, bf16[2,128]{1,0:T(2,128)(2,1)} %bitcast.11, ...), custom_call_target="tpu_custom_call" | custom-call | flops 4294967296 | bytes 4194304 | tf_op jit(solution)/shard_map/pallas_call | solution.py:645
  82.3 2.3 %shard_map.111 = (bf16[32,128]{1,0:T(8,128)(2,1)}, f32[2,128]{1,0:T(2,128)}, bf16[1,2048,128]{2,1,0:T(8,128)(2,1)}, bf16[1,2048,128]{2,1,0:T(8,128)(2,1)}, bf16[1,128,2048]{2,1,0:T(8,128)(2,1)}) custom-call(bf16[32,128]{1,0:T(8,128)(2,1)} %get-tuple-element.15.refs_0_, f32[2,128]{1,0:T(2,128)} %get-tuple-element.16.refs_1_, ...), custom_call_target="tpu_custom_call" | custom-call | tf_op jit(solution)/shard_map/pallas_call | solution.py:663
